TPU v7x, 32 devices: a whole 2x2x4 slice. The times are simulated.
32 devices in a mesh: section: 4 (over y, x), frame: 2 (over core), patch: 4 (over z).
Axes of the slice: x: 2, y: 2, z: 4, core: 2. Of those that a mesh axis runs over, the one named last changes fastest.
Arguments:
- exposure: bfloat16 [2, 2, 896, 4096], P('frame', None, ('section', 'patch')), may hold values from -6 to 6, as said below
- row_prof: bfloat16 [2, 320, 50, 64], P('frame', ('section', 'patch')), may hold values from -0.875 to 0.875
- col_prof: bfloat16 [2, 320, 25, 256], P('frame', ('section', 'patch')), may hold values from -1.25 to 1.25
- row_off: int32 [2, 320], P('frame', ('section', 'patch')), may hold values from 0 to 8, as said below
- col_off: int32 [2, 320], P('frame', ('section', 'patch')), may hold values from 0 to 3840, as said below
- dest: int32 [2, 320], P('frame', ('section', 'patch')), may hold values from 0 to 3, as said below
- fibre_weight: float32 [2, 320, 25], P('frame', ('section', 'patch')), may hold values from 0.2 to 5
Outputs:
- spectra_ext: float32 [2, 320, 50, 25], P('frame', ('section', 'patch'))
- coadd: float32 [320, 50, 25], P(('section', 'patch'))
Inputs may be any that keep to these rules, and one draw needn't show every extreme that they name: `exposure`: channel 0 holds pixel values, channel 1 inverse variances between 0.25 and 4. `row_off`: offsets of patches within their band extended by 8 rows on each side. `col_off`: patches of neighbouring fibre blocks share columns. `dest`: of the 20 patches of one band (p // 20 equal) in one frame, each patch index receives 20 // 4 or (23) // 4 of them, so at most 5, and some index exactly 5.
All inputs are finite; a program needn't handle non-finite values.
Results may differ from a plain program's by a relative error of at most 0.0003.
Values may be sent and summed in bfloat16 or wider, within the bound.
No kernel may reach another device: no remote copies, remote signals or barrier semaphores. Data moves between devices by JAX's collectives and lax.ppermute only.
A program may use at most 64 MiB of HBM per device.

v0:
```python
import functools

import jax
import jax.numpy as jnp
from jax import lax
from jax.experimental import pallas as pl
from jax.experimental.pallas import tpu as pltpu
from jax.sharding import PartitionSpec as P

HALO = 8
PC = 256
ITERS = 6
PR = 64
LANES = 128
SUB = 8
HALF = LANES // 2
CODE_BITS = 15.0
CODE_TOP = 32767.0
TINY = 1e-30
EDGE_FLOPS = 1 << 34
EDGE_BYTES = 1 << 27
F32 = jnp.float32
BF16 = jnp.bfloat16


def up(count, multiple):
    return -(-count // multiple) * multiple


def dot_nt(lhs, rhs):
    return lax.dot_general(lhs, rhs, (((1,), (1,)), ((), ())), preferred_element_type=F32)


def dot_nn(lhs, rhs):
    return lax.dot_general(lhs, rhs, (((1,), (0,)), ((), ())), preferred_element_type=F32)


def two_parts(value):
    high = value.astype(BF16)
    return high, (value - high.astype(F32)).astype(BF16)


def two_pass(dot, value, weights):
    rows = value.shape[0]
    both = dot(jnp.concatenate(two_parts(value), axis=0), weights)
    return both[:rows] + both[rows:]


def block_tiles(fibres):
    blocks = fibres // SUB
    tiles = [(f, t) for f in range(blocks * SUB) for t in range(f // SUB, blocks)]
    for f in range(blocks * SUB, fibres):
        tiles += [(f, t) for t in range(up(fibres, SUB) // SUB)]
    return tiles


def split_lanes(value):
    return [value[:, at : at + LANES] for at in range(0, value.shape[1], LANES)]


def shifted(pieces, shift):
    rows = pieces[0].shape[0]
    turned = [pltpu.roll(piece, LANES - shift, 1) for piece in pieces]
    inside = lax.broadcasted_iota(jnp.int32, (rows, LANES), 1) < LANES - shift
    return [jnp.where(inside, turned[i], turned[i + 1]) for i in range(len(pieces) - 1)]


def start_copies(sources, targets, arrived):
    copies = [
        pltpu.make_async_copy(source, target, arrived.at[index])
        for index, (source, target) in enumerate(zip(sources, targets))
    ]
    for copy in copies:
        copy.start()
    return copies


def prepare_kernel(
    row_off_in,
    col_off_in,
    exposure,
    row_prof,
    col_prof,
    weight,
    products,
    weights_w,
    upper_wx,
    lower_wx,
    fibre,
    row_block,
    weight_lanes,
    row_off,
    col_off,
    band_w,
    band_wx,
    prof,
    fibre_rows,
    cut_row,
    arrived,
):
    copies = start_copies((row_off_in, col_off_in), (row_off, col_off), arrived)
    patches, waves, _ = row_prof.shape
    fibres = col_prof.shape[0]
    columns = exposure.shape[2]
    padded_p = up(patches, SUB)
    tiles = block_tiles(fibres)
    inverse = exposure[1].astype(F32)
    scaled = inverse * exposure[0].astype(F32)
    for piece, value in enumerate(split_lanes(inverse)):
        band_w[piece] = value
    for piece, value in enumerate(split_lanes(scaled)):
        band_wx[piece] = value
    for f in range(fibres):
        for piece, value in enumerate(split_lanes(col_prof[f].astype(F32))):
            prof[piece, f * padded_p : f * padded_p + patches, :] = value
    for copy in copies:
        copy.wait()
    cut_row[...] = jnp.zeros_like(cut_row)
    fibre_rows[...] = jnp.zeros_like(fibre_rows)
    halo = jnp.zeros((HALO, LANES), F32)
    square = (fibre.shape[1], fibres)
    eye = lax.broadcasted_iota(jnp.int32, square, 0) == lax.broadcasted_iota(jnp.int32, square, 1)
    lower_half = lax.broadcasted_iota(jnp.int32, (HALF, LANES), 1) < HALF

    def prepare(patch, carry):
        first_row = row_off[patch]
        first_col = col_off[patch]
        base = first_col // LANES
        shift = first_col - base * LANES
        count = PC // LANES
        window = shifted([band_w[base + piece] for piece in range(count + 1)], shift)
        for piece, value in enumerate(window):
            lanes = slice(piece * LANES, (piece + 1) * LANES)
            weights_w[patch, :, lanes] = jnp.concatenate([halo, value], axis=0).astype(BF16)
        window = shifted([band_wx[base + piece] for piece in range(count + 1)], shift)
        for piece, value in enumerate(window):
            lanes = slice(piece * LANES, (piece + 1) * LANES)
            upper, lower = two_parts(jnp.concatenate([halo, value], axis=0))
            upper_wx[patch, :, lanes] = upper
            lower_wx[patch, :, lanes] = lower
        for piece in range(count):
            lanes = slice(piece * LANES, (piece + 1) * LANES)
            fibre_rows[0:fibres, lanes] = prof[piece, pl.ds(patch, fibres, stride=padded_p), :]
        fibre[patch] = fibre_rows[...].astype(BF16)
        for at in range(0, len(tiles), 2):
            value = jnp.concatenate(
                [
                    fibre_rows[f : f + 1, :] * fibre_rows[t * SUB : (t + 1) * SUB, :]
                    for f, t in tiles[at : at + 2]
                ],
                axis=0,
            )
            upper, lower = two_parts(value)
            products[patch, at * SUB : (at + 2) * SUB, 0:PC] = upper
            products[patch, at * SUB : (at + 2) * SUB, PC : 2 * PC] = lower
        cut_row[0:waves, 0:PR] = row_prof[patch].astype(F32)
        profile = cut_row[...]
        turned = pltpu.roll(profile + pltpu.roll(profile, HALF, 1), first_row, 1)
        keep = lower_half == (lax.rem(patch, 2) == 0)
        row_block[patch] = jnp.where(keep, turned, 0.0).astype(BF16)
        own = jnp.broadcast_to(weight[patch], eye.shape)
        own = jnp.sum(jnp.where(eye, own, 0.0), axis=1, keepdims=True)
        weight_lanes[patch] = jnp.where(keep[: own.shape[0]], own, 0.0)
        return carry

    lax.fori_loop(0, patches, prepare, 0)


def solve_kernel(
    fibres,
    waves,
    row_off_in,
    col_off_in,
    dest_in,
    halo_one,
    halo_near,
    halo_far,
    products,
    weights_w,
    upper_wx,
    lower_wx,
    fibre,
    row_block,
    weight_lanes,
    send,
    numer,
    row_off,
    col_off,
    dest,
    halo_w,
    halo_wx,
    top_w,
    top_upper,
    top_lower,
    matrix,
    tails,
    estimate,
    residual,
    direction,
    imaged,
    across,
    partial,
    norm,
    packed,
    counts,
    arrived,
):
    copies = start_copies(
        (row_off_in, col_off_in, dest_in), (row_off, col_off, dest), arrived
    )
    patches = products.shape[0]
    pairs = patches // 2
    blocks = fibres // SUB
    main = blocks * SUB
    padded_f = up(fibres, SUB)
    tiles = block_tiles(fibres)
    rank = lax.axis_index("section") * lax.axis_size("patch") + lax.axis_index("patch")
    odd = lax.rem(rank, 2) == 1

    for slot, sources in enumerate(((halo_one,), (halo_near, halo_far))):
        rows = slice(slot * HALO, (slot + 1) * HALO)
        values, inverse = (
            sum(source[channel].astype(F32) for source in sources) for channel in range(2)
        )
        for piece, value in enumerate(split_lanes(inverse)):
            halo_w[piece, rows, :] = value
        for piece, value in enumerate(split_lanes(inverse * values)):
            halo_wx[piece, rows, :] = value
    partial[...] = jnp.zeros_like(partial)
    halo_row = lax.broadcasted_iota(jnp.int32, (HALO, LANES), 0)
    empty = jnp.zeros((PR, PC), BF16)
    copies[0].wait()
    copies[1].wait()

    def beside_own(edge, own):
        return jnp.concatenate([edge, own.astype(F32)[HALO:]], axis=0).astype(BF16)

    for patch in range(patches):
        first_row = row_off[patch]
        first_col = col_off[patch]
        base = first_col // LANES
        shift = first_col - base * LANES
        take_one = (halo_row >= first_row) == odd
        edges = []
        for source in (halo_w, halo_wx):
            pieces = [
                jnp.where(
                    take_one,
                    source[base + piece, 0:HALO, :],
                    source[base + piece, HALO : 2 * HALO, :],
                )
                for piece in range(PC // LANES + 1)
            ]
            edges.append(jnp.concatenate(shifted(pieces, shift), axis=1))
        above = edges[1].astype(BF16).astype(F32)
        top_w[patch] = beside_own(edges[0], weights_w[patch, : 2 * HALO, :])
        top_upper[patch] = beside_own(above, upper_wx[patch, : 2 * HALO, :])
        top_lower[patch] = beside_own(edges[1] - above, lower_wx[patch, : 2 * HALO, :])

    halves = partial.shape[0]
    members = [list(range(at, pairs, halves)) for at in range(halves)]

    def set_partial(pair, value):
        row = pair // halves
        partial[pair % halves, row : row + 1, :] = value

    def whole(top, own, patch):
        return jnp.concatenate([top[patch], own[patch, 2 * HALO :, :]], axis=0)

    def diagonal(first, second):
        return jnp.concatenate(
            [
                jnp.concatenate(first + [empty] * len(second), axis=1),
                jnp.concatenate([empty] * len(first) + second, axis=1),
            ],
            axis=0,
        )

    for pair in range(pairs):
        one, two = 2 * pair, 2 * pair + 1
        folded = dot_nt(
            jnp.concatenate([fibre[one], fibre[one], fibre[two], fibre[two]], axis=1),
            diagonal(
                [whole(top_upper, upper_wx, one), whole(top_lower, lower_wx, one)],
                [whole(top_upper, upper_wx, two), whole(top_lower, lower_wx, two)],
            ),
        )
        imaged[pair] = folded
    for pair in range(pairs):
        rhs = two_pass(dot_nt, imaged[pair], row_block[pair])
        residual[pair] = rhs
        direction[pair] = rhs
        estimate[pair] = jnp.zeros_like(rhs)
        set_partial(pair, jnp.sum(rhs * rhs, axis=0, keepdims=True))
    for pair in range(pairs):
        one, two = 2 * pair, 2 * pair + 1
        blended = dot_nt(
            jnp.concatenate([products[one], products[two]], axis=1),
            diagonal(
                [whole(top_w, weights_w, one)] * 2,
                [whole(top_w, weights_w, two)] * 2,
            ),
        )
        for index, (f, t) in enumerate(tiles):
            value = blended[index * SUB : (index + 1) * SUB]
            if f < main:
                matrix[pair, f * main + t * SUB : f * main + (t + 1) * SUB, :] = value
                if t > f // SUB:
                    matrix[pair, pl.ds(t * SUB * main + f, SUB, stride=main), :] = value
            else:
                if t < blocks:
                    matrix[pair, f * main + t * SUB : f * main + (t + 1) * SUB, :] = value
                tails[pair, f - main, t * SUB : (t + 1) * SUB, :] = value

    lower_half = lax.broadcasted_iota(jnp.int32, partial.shape[1:], 1) < HALF

    def patch_sums(value):
        first = jnp.sum(jnp.where(lower_half, value, 0.0), axis=1, keepdims=True)
        second = jnp.sum(jnp.where(lower_half, 0.0, value), axis=1, keepdims=True)
        return jnp.where(lower_half, first, second)

    def apply(dot, source, target, some):
        sides = [jnp.concatenate(two_parts(source[pair]), axis=0) for pair in some]
        blocks = [row_block[pair] for pair in some]
        if len(some) > 1:
            none = jnp.zeros_like(blocks[0])
            blocks = [
                jnp.concatenate(
                    [block if here == there else none for there in range(len(some))], axis=1
                )
                for here, block in enumerate(blocks)
            ]
        both = dot(jnp.concatenate(sides, axis=1), jnp.concatenate(blocks, axis=0))
        for index, pair in enumerate(some):
            lanes = both[:, index * LANES : (index + 1) * LANES]
            target[pair] = lanes[:padded_f] + lanes[padded_f:]

    def blend(pair):
        totals = [jnp.zeros((main, LANES), F32)] * 2
        for f in range(fibres):
            totals[f % 2] = totals[f % 2] + (
                matrix[pair, f * main : (f + 1) * main, :] * across[pair, f : f + 1, :]
            )
        total = totals[0] + totals[1]
        imaged[pair, 0:main, :] = total
        product = jnp.sum(total * across[pair, 0:main, :], axis=0, keepdims=True)
        if fibres > main:
            rest = jnp.zeros((padded_f - main, LANES), F32)
            row = lax.broadcasted_iota(jnp.int32, rest.shape, 0)
            for f in range(main, fibres):
                one = jnp.sum(tails[pair, f - main] * across[pair], axis=0, keepdims=True)
                rest = jnp.where(row == f - main, one, rest)
                product = product + one * across[pair, f : f + 1, :]
            imaged[pair, main:padded_f, :] = rest
        set_partial(pair, product)

    def image(half, folded=True):
        some = [members[half][at : at + 2] for at in range(0, len(members[half]), 2)]
        for turn in range(len(some) + 2):
            if turn < len(some):
                apply(dot_nn, direction, across, some[turn])
            if 0 <= turn - 1 < len(some):
                for pair in some[turn - 1]:
                    blend(pair)
            if folded and 0 <= turn - 2:
                apply(dot_nt, imaged, imaged, some[turn - 2])

    def advance(half):
        curvature = patch_sums(partial[half])
        step_size = norm[half] / jnp.where(curvature > 0.0, curvature, 1.0)
        sizes = [step_size[row : row + 1] for row in range(len(members[half]))]
        for size, pair in zip(sizes, members[half]):
            estimate[pair] = estimate[pair] + size * direction[pair]
        return sizes

    def move(half):
        sizes = advance(half)
        for size, pair in zip(sizes, members[half]):
            rest = residual[pair] - size * imaged[pair]
            residual[pair] = rest
            set_partial(pair, jnp.sum(rest * rest, axis=0, keepdims=True))
        norm_now = norm[half]
        norm_next = patch_sums(partial[half])
        ratio = norm_next / jnp.where(norm_now > 0.0, norm_now, 1.0)
        for row, pair in enumerate(members[half]):
            direction[pair] = residual[pair] + ratio[row : row + 1] * direction[pair]
        norm[half] = norm_next

    for half in range(halves):
        norm[half] = patch_sums(partial[half])
    image(0)
    image(1)
    move(0)

    def turn_about(step, carry):
        image(0)
        move(1)
        image(1)
        move(0)
        return carry

    lax.fori_loop(0, ITERS - 2, turn_about, 0)
    image(0, folded=False)
    move(1)
    image(1, folded=False)
    advance(0)
    advance(1)

    copies[2].wait()
    for index in range(send.shape[0]):
        counts[index] = 0
    packed[...] = jnp.zeros_like(packed)
    upper_rows = (fibres + 1) // 2
    lane_f = lax.broadcasted_iota(jnp.int32, (padded_f, LANES), 1)
    at_wave = lax.rem(lane_f, HALF) == waves
    unit = jnp.where(at_wave, 1.0, 0.0)
    for pair in range(pairs):
        spectra = estimate[pair]
        numer[pair] = (spectra + unit) * (weight_lanes[2 * pair] + weight_lanes[2 * pair + 1])
        size = jnp.abs(spectra)
        first = jnp.max(jnp.where(lane_f < HALF, size, 0.0), axis=1, keepdims=True)
        second = jnp.max(jnp.where(lane_f < HALF, 0.0, size), axis=1, keepdims=True)
        largest = jnp.where(lane_f < HALF, first, second)
        power = jnp.floor(jnp.log2(jnp.maximum(largest, TINY))) + 1.0
        coded = jnp.clip(jnp.round(spectra * jnp.exp2(CODE_BITS - power)), -CODE_TOP, CODE_TOP)
        coded = jnp.where(at_wave, power, coded)
        turned = pltpu.roll(coded, HALF, 1)
        for half in range(2):
            here = turned if half else coded
            away = coded if half else turned
            target = dest[2 * pair + half]
            slot = counts[target]
            counts[target] = slot + 1
            compact = jnp.where(
                lane_f[:upper_rows] < HALF,
                here[:upper_rows],
                jnp.concatenate(
                    [away[upper_rows:fibres], away[: 2 * upper_rows - fibres]], axis=0
                ),
            )
            packed[target, pl.ds(slot * upper_rows, upper_rows), :] = compact
    for index in range(send.shape[0]):
        send[index] = packed[index].astype(jnp.int32).astype(jnp.int16)


def finish_kernel(
    capacity, received, numer, others, spectra_out, coadd_out, spectra_ext, coadd, collected, sent
):
    fibres, patches, waves = coadd.shape
    padded_p = up(patches, SUB)
    lower_half = lax.broadcasted_iota(jnp.int32, numer.shape[1:], 1) < HALF
    for pair in range(numer.shape[0]):
        total = numer[pair]
        for index in range(others.shape[0]):
            total = total + others[index, pair]
        first, second = total[:, waves : waves + 1], total[:, HALF + waves : HALF + waves + 1]
        mean = total / jnp.where(lower_half, first, second)
        for half in range(2):
            value = pltpu.roll(mean, HALF, 1) if half else mean
            collected[pl.ds(2 * pair + half, fibres, stride=padded_p), :] = value[:fibres]
    for f in range(fibres):
        coadd[f] = collected[f * padded_p : f * padded_p + patches, :waves]
    copies = [pltpu.make_async_copy(coadd, coadd_out, sent.at[0])]
    copies[0].start()
    upper_rows = (fibres + 1) // 2
    lower_half = lax.broadcasted_iota(jnp.int32, received.shape[1:], 1) < HALF
    for source in range(received.shape[0]):
        coded = received[source].astype(jnp.int32).astype(F32)
        power = jnp.where(
            lower_half, coded[:, waves : waves + 1], coded[:, HALF + waves : HALF + waves + 1]
        )
        value = coded * jnp.exp2(power - CODE_BITS)
        turned = pltpu.roll(value, HALF, 1)
        for slot in range(capacity):
            entry = source * capacity + slot
            at = slot * upper_rows
            spectra_ext[entry, 0:upper_rows, 0, :] = value[at : at + upper_rows, :waves]
            at_end = at + fibres - upper_rows
            spectra_ext[entry, upper_rows:fibres, 0, :] = turned[at:at_end, :waves]
        entries = pl.ds(source * capacity, capacity)
        copy = pltpu.make_async_copy(
            spectra_ext.at[entries], spectra_out.at[entries], sent.at[1 + source]
        )
        copy.start()
        copies.append(copy)
    for copy in copies:
        copy.wait()


def vmem(count=1):
    return [pl.BlockSpec(memory_space=pltpu.VMEM)] * count


def hbm(count=1):
    return [pl.BlockSpec(memory_space=pltpu.HBM)] * count


def prepare(exposure, row_prof, col_prof, row_off, col_off, weight):
    patches = row_prof.shape[0]
    fibres = col_prof.shape[0]
    _, band, columns = exposure.shape
    padded_f = up(fibres, SUB)
    padded_p = up(patches, SUB)
    rows = SUB * len(block_tiles(fibres))

    def made(*shape):
        return jax.ShapeDtypeStruct((patches,) + shape, BF16)

    return list(
        pl.pallas_call(
        prepare_kernel,
        out_shape=(
            made(rows, 2 * PC),
            made(PR, PC),
            made(PR, PC),
            made(PR, PC),
            made(padded_f, PC),
            made(HALF, LANES),
            jax.ShapeDtypeStruct((patches, padded_f, LANES), F32),
        ),
        in_specs=hbm(2) + vmem(4),
        out_specs=tuple(vmem(7)),
        scratch_shapes=[
            pltpu.SMEM(row_off.shape, row_off.dtype),
            pltpu.SMEM(col_off.shape, col_off.dtype),
            pltpu.VMEM((columns // LANES + 1, band, LANES), F32),
            pltpu.VMEM((columns // LANES + 1, band, LANES), F32),
            pltpu.VMEM((PC // LANES, fibres * padded_p, LANES), F32),
            pltpu.VMEM((padded_f, PC), F32),
            pltpu.VMEM((HALF, LANES), F32),
            pltpu.SemaphoreType.DMA((2,)),
        ],
        cost_estimate=pl.CostEstimate(
            flops=patches * rows * PC * 8, bytes_accessed=16 * 1024 * 1024, transcendentals=0
        ),
        compiler_params=pltpu.CompilerParams(vmem_limit_bytes=24 * 1024 * 1024),
    )(row_off, col_off, exposure, row_prof, col_prof, weight)
    )


def solve(halos, prepared, fibres, waves, row_off, col_off, dest, group):
    patches = dest.shape[0]
    columns = halos[0].shape[2]
    capacity = (patches + group - 1) // group
    pairs = patches // 2
    main = fibres // SUB * SUB
    padded_f = up(fibres, SUB)
    code_rows = up(capacity * ((fibres + 1) // 2), SUB)
    vectors = pltpu.VMEM((pairs, padded_f, LANES), F32)
    sums = pltpu.VMEM((2, up((pairs + 1) // 2, SUB), LANES), F32)
    tops = pltpu.VMEM((patches, 2 * HALO, PC), BF16)
    halo_band = pltpu.VMEM((columns // LANES + 1, 2 * HALO, LANES), F32)
    return pl.pallas_call(
        functools.partial(solve_kernel, fibres, waves),
        out_shape=(
            jax.ShapeDtypeStruct((group, code_rows, LANES), jnp.int16),
            jax.ShapeDtypeStruct((pairs, padded_f, LANES), F32),
        ),
        in_specs=hbm(3) + vmem(10),
        out_specs=tuple(vmem(2)),
        scratch_shapes=[
            pltpu.SMEM(row_off.shape, row_off.dtype),
            pltpu.SMEM(col_off.shape, col_off.dtype),
            pltpu.SMEM(dest.shape, dest.dtype),
            halo_band,
            halo_band,
            tops,
            tops,
            tops,
            pltpu.VMEM((pairs, fibres * main, LANES), F32),
            pltpu.VMEM((pairs, max(fibres - main, 1), padded_f, LANES), F32),
            vectors,
            vectors,
            vectors,
            vectors,
            vectors,
            sums,
            sums,
            pltpu.VMEM((group, code_rows, LANES), F32),
            pltpu.SMEM((group,), jnp.int32),
            pltpu.SemaphoreType.DMA((3,)),
        ],
        compiler_params=pltpu.CompilerParams(vmem_limit_bytes=24 * 1024 * 1024),
    )(row_off, col_off, dest, *halos, *prepared)


def finish(received, numer, others, capacity, patches, fibres, waves):
    entries = received.shape[0] * capacity
    return pl.pallas_call(
        functools.partial(finish_kernel, capacity),
        out_shape=(
            jax.ShapeDtypeStruct((entries, fibres, 1, waves), F32),
            jax.ShapeDtypeStruct((fibres, patches, waves), F32),
        ),
        in_specs=vmem(3),
        out_specs=tuple(hbm(2)),
        scratch_shapes=[
            pltpu.VMEM((entries, fibres, 1, waves), F32),
            pltpu.VMEM((fibres, patches, waves), F32),
            pltpu.VMEM((fibres * up(patches, SUB), LANES), F32),
            pltpu.SemaphoreType.DMA((1 + received.shape[0],)),
        ],
        compiler_params=pltpu.CompilerParams(vmem_limit_bytes=16 * 1024 * 1024),
    )(received, numer, others)


def edge_kernel(exposure, two, one):
    rank = lax.axis_index("section") * lax.axis_size("patch") + lax.axis_index("patch")
    even = lax.rem(rank, 2) == 0
    band = exposure.shape[1]
    for channel in range(exposure.shape[0]):
        top = exposure[channel, 0:HALO, :].astype(F32)
        bottom = exposure[channel, band - HALO : band, :].astype(F32)
        one[channel] = jnp.where(even, bottom, top).astype(BF16)
        two[channel] = jnp.where(even, top, bottom).astype(BF16)


def edges(exposure):
    channels, _, columns = exposure.shape
    return pl.pallas_call(
        edge_kernel,
        out_shape=(jax.ShapeDtypeStruct((channels, HALO, columns), BF16),) * 2,
        in_specs=vmem(1),
        out_specs=tuple(vmem(2)),
        cost_estimate=pl.CostEstimate(
            flops=EDGE_FLOPS, bytes_accessed=EDGE_BYTES, transcendentals=0
        ),
        compiler_params=pltpu.CompilerParams(vmem_limit_bytes=8 * 1024 * 1024),
    )(exposure)


def neighbours(block):
    axes = ("section", "patch")
    count = lax.axis_size(axes)
    group = lax.axis_size("patch")
    two, one = edges(block)

    def exchange(value, firsts):
        pairs = [(i, i + 1) for i in firsts if i + 1 < count]
        return lax.ppermute(value, axes, pairs + [(b, a) for a, b in pairs])

    odd = range(1, count, 2)
    far = [i for i in odd if (i + 1) % group == 0]
    near = [i for i in odd if (i + 1) % group]
    return [exchange(one, range(0, count, 2)), exchange(two, near), exchange(two, far)]


def local(exposure, row_prof, col_prof, row_off, col_off, dest, fibre_weight):
    group = lax.axis_size("patch")
    frames = lax.axis_size("frame")
    patches = dest.shape[1]
    fibres, waves = col_prof.shape[2], row_prof.shape[2]
    capacity = (patches + group - 1) // group
    halos = neighbours(exposure[0])
    prepared = prepare(
        exposure[0],
        row_prof[0],
        col_prof[0].transpose(1, 0, 2),
        row_off[0],
        col_off[0],
        fibre_weight[0][:, None, :],
    )
    prepared[5] = prepared[5].reshape(patches // 2, LANES, LANES)
    send, numer = solve(halos, prepared, fibres, waves, row_off[0], col_off[0], dest[0], group)
    received = lax.all_to_all(send, "patch", split_axis=0, concat_axis=0, tiled=True)
    others = jnp.stack(
        [
            lax.ppermute(numer, "frame", [(i, (i + hop) % frames) for i in range(frames)])
            for hop in range(1, frames)
        ]
    )
    spectra_ext, coadd = finish(received, numer, others, capacity, patches, fibres, waves)
    return spectra_ext.transpose(2, 0, 3, 1), coadd.transpose(1, 2, 0)


def solution(mesh):
    in_specs = (
        P("frame", None, ("section", "patch"), None),
        P("frame", ("section", "patch"), None, None),
        P("frame", ("section", "patch"), None, None),
        P("frame", ("section", "patch")),
        P("frame", ("section", "patch")),
        P("frame", ("section", "patch")),
        P("frame", ("section", "patch"), None),
    )
    out_specs = (P("frame", ("section", "patch"), None, None), P(("section", "patch"), None, None))
    return jax.shard_map(local, mesh=mesh, in_specs=in_specs, out_specs=out_specs, check_vma=False)
```

profile of v0, /device:TPU:0, one launch (start us, length us, event | category | flops | bytes accessed | tf_op | source)
XLA Modules:
  0.0 34.3 jit_solution(11408168727698567809)
XLA Ops:
  0.6 0.0 copy-start
  0.6 1.2 %copy-done = bf16[1,2,56,4096]{3,2,1,0:T(8,128)(2,1)S(1)} copy-done((bf16[1,2,56,4096]{3,2,1,0:T(8,128)(2,1)S(1)}, bf16[1,2,56,4096]{3,2,1,0:T(8,128)(2,1)}, u32[]{:S(2)}) %copy-start) | copy-done | bytes 917528
  1.8 0.0 copy-start.5
  1.8 0.0 copy-start.6
  1.8 0.0 copy-start.7
  1.9 0.1 shard_map.86
  1.9 3.1 %collective-permute-start = (bf16[2,8,4096]{2,1,0:T(8,128)(2,1)S(1)}, bf16[2,8,4096]{2,1,0:T(8,128)(2,1)S(1)}, u32[]{:S(2)}, u32[]{:S(2)}) collective-permute-start(bf16[2,8,4096]{2,1,0:T(8,128)(2,1)S(1)} %get-tuple-element.15), channel_id=1, source_target_pairs={{0,1},{2,3},{8,9},{10,11},{16,17},{18,19},{24,25},{26,27},{1,0},{3... | collective-permute-start | bytes 393224 | tf_op jit(solution)/shard_map/ppermute | solution.py:640
  5.0 0.7 %collective-permute-start.2 = (bf16[2,8,4096]{2,1,0:T(8,128)(2,1)S(1)}, bf16[2,8,4096]{2,1,0:T(8,128)(2,1)S(1)}, u32[]{:S(2)}, u32[]{:S(2)}) collective-permute-start(bf16[2,8,4096]{2,1,0:T(8,128)(2,1)S(1)} %get-tuple-element.16), channel_id=1, source_target_pairs={{3,8},{11,16},{19,24},{8,3},{16,11},{24,19},{7,12},{15,20},{23,28}... | collective-permute-start | bytes 393224 | tf_op jit(solution)/shard_map/ppermute | solution.py:640
  5.7 0.7 %collective-permute-start.1 = (bf16[2,8,4096]{2,1,0:T(8,128)(2,1)S(1)}, bf16[2,8,4096]{2,1,0:T(8,128)(2,1)S(1)}, u32[]{:S(2)}, u32[]{:S(2)}) collective-permute-start(bf16[2,8,4096]{2,1,0:T(8,128)(2,1)S(1)} %get-tuple-element.16), channel_id=1, source_target_pairs={{1,2},{9,10},{17,18},{25,26},{2,1},{10,9},{18,17},{26,25},{5,6},{1... | collective-permute-start | bytes 393224 | tf_op jit(solution)/shard_map/ppermute | solution.py:640
  6.4 0.0 copy-done.1
  6.4 0.0 copy-done.2
  6.4 0.0 copy-done.3
  6.4 0.0 copy-done.4
  6.4 0.0 copy-done.5
  6.4 0.0 copy-done.6
  6.4 3.7 %shard_map.87 = (bf16[20,416,512]{2,1,0:T(8,128)(2,1)S(1)}, bf16[20,64,256]{2,1,0:T(8,128)(2,1)S(1)}, bf16[20,64,256]{2,1,0:T(8,128)(2,1)S(1)}, bf16[20,64,256]{...) custom-call(s32[20]{0:T(128)S(1)} %bitcast.20, ...), custom_call_target="tpu_custom_call" | custom-call | flops 17039360 | bytes 16777216 | tf_op jit(solution)/shard_map/pallas_call | solution.py:510
  10.1 0.0 collective-permute-done.halo_one
  10.1 0.0 collective-permute-done.2.halo_far
  10.2 0.0 collective-permute-done.1.halo_near
  10.2 8.4 %shard_map.88 = (s16[4,72,128]{2,1,0:T(8,128)(2,1)S(1)}, f32[10,32,128]{2,1,0:T(8,128)S(1)}) custom-call(s32[20]{0:T(128)S(1)} %bitcast.21, s32[20]{0:T(128)S(1)} %bitcast.23, s32[20]{0:T(128)S(1)} %bitcast.24, bf16[2,8,4096]{2,1,0:T(8,128)(2,1)S(1)} %collective-permute-done.halo_one, bf16[2,8,4096]{2,1,0:T(8,128)(2,1)S(1)} %collective-permute-done.1.halo_near, ...), custom_call_target="tpu_custom_call" | custom-call | tf_op jit(solution)/shard_map/pallas_call | solution.py:553
  18.6 0.1 collective-permute-start.3
  18.7 13.9 %all_to_all.5.received = s16[4,72,128]{2,1,0:T(8,128)(2,1)S(1)} all-to-all(s16[4,72,128]{2,1,0:T(8,128)(2,1)S(1)} %get-tuple-element.24), channel_id=1, replica_groups=mesh['section'=4,'frame'=2,'patch'=4] {'patch'}, dimensions={0} | all-to-all | bytes 147456 | tf_op jit(solution)/shard_map/all_to_all | solution.py:665
  32.7 0.0 collective-permute-done.3
  32.7 1.6 %shard_map.89 = (f32[20,25,1,50]{3,2,1,0:T(1,128)}, f32[25,20,50]{2,1,0:T(8,128)}) custom-call(s16[4,72,128]{2,1,0:T(8,128)(2,1)S(1)} %all_to_all.5.received, f32[10,32,128]{2,1,0:T(8,128)S(1)} %get-tuple-element.25.numer, f32[1,10,32,128]{3,2,1,0:T(8,128)S(1)} %bitcast.18), custom_call_target="tpu_custom_call" | custom-call | tf_op jit(solution)/shard_map/pallas_call | solution.py:589
  (5 shorter events, 0.0 us)
Async XLA Ops:
  0.6 1.2 %copy-start = (bf16[1,2,56,4096]{3,2,1,0:T(8,128)(2,1)S(1)}, bf16[1,2,56,4096]{3,2,1,0:T(8,128)(2,1)}, u32[]{:S(2)}) copy-start(bf16[1,2,56,4096]{3,2,1,0:T(8,128)(2,1)} %param.7) | copy-start | bytes 2752516
  1.8 4.6 %copy-start.1 = (bf16[1,2,56,4096]{3,2,1,0:T(8,128)(2,1)S(1)}, bf16[1,2,56,4096]{3,2,1,0:T(8,128)(2,1)}, u32[]{:S(2)}) copy-start(bf16[1,2,56,4096]{3,2,1,0:T(8,128)(2,1)} %param.7) | copy-start | bytes 2752516
  1.8 4.6 %copy-start.2 = (bf16[1,20,25,256]{3,1,2,0:T(8,128)(2,1)S(1)}, bf16[1,20,25,256]{3,1,2,0:T(8,128)(2,1)}, u32[]{:S(2)}) copy-start(bf16[1,20,25,256]{3,1,2,0:T(8,128)(2,1)} %param.9) | copy-start | bytes 768004
  1.8 4.6 %copy-start.3 = (bf16[1,20,50,64]{3,2,1,0:T(8,128)(2,1)S(1)}, bf16[1,20,50,64]{3,2,1,0:T(8,128)(2,1)}, u32[]{:S(2)}) copy-start(bf16[1,20,50,64]{3,2,1,0:T(8,128)(2,1)} %param.8) | copy-start | bytes 384004
  1.8 4.6 %copy-start.4 = (f32[1,20,25]{2,0,1:T(1,128)S(1)}, f32[1,20,25]{2,0,1:T(1,128)}, u32[]{:S(2)}) copy-start(f32[1,20,25]{2,0,1:T(1,128)} %param.13) | copy-start | bytes 6004
  1.8 4.6 %copy-start.5 = (s32[1,20]{1,0:T(1,128)S(1)}, s32[1,20]{1,0:T(1,128)}, u32[]{:S(2)}) copy-start(s32[1,20]{1,0:T(1,128)} %param.10) | copy-start | bytes 244
  1.8 4.6 %copy-start.6 = (s32[1,20]{1,0:T(1,128)S(1)}, s32[1,20]{1,0:T(1,128)}, u32[]{:S(2)}) copy-start(s32[1,20]{1,0:T(1,128)} %param.11) | copy-start | bytes 244
  1.8 8.3 %copy-start.7 = (s32[1,20]{1,0:T(1,128)S(1)}, s32[1,20]{1,0:T(1,128)}, u32[]{:S(2)}) copy-start(s32[1,20]{1,0:T(1,128)} %param.12) | copy-start | bytes 244
  1.9 8.2 %collective-permute-start = (bf16[2,8,4096]{2,1,0:T(8,128)(2,1)S(1)}, bf16[2,8,4096]{2,1,0:T(8,128)(2,1)S(1)}, u32[]{:S(2)}, u32[]{:S(2)}) collective-permute-start(bf16[2,8,4096]{2,1,0:T(8,128)(2,1)S(1)} %get-tuple-element.15), channel_id=1, source_target_pairs={{0,1},{2,3},{8,9},{10,11},{16,17},{18,19},{24,25},{26,27},{1,0},{3... | collective-permute-start | bytes 393224 | tf_op jit(solution)/shard_map/ppermute | solution.py:640
  5.0 5.1 %collective-permute-start.2 = (bf16[2,8,4096]{2,1,0:T(8,128)(2,1)S(1)}, bf16[2,8,4096]{2,1,0:T(8,128)(2,1)S(1)}, u32[]{:S(2)}, u32[]{:S(2)}) collective-permute-start(bf16[2,8,4096]{2,1,0:T(8,128)(2,1)S(1)} %get-tuple-element.16), channel_id=1, source_target_pairs={{3,8},{11,16},{19,24},{8,3},{16,11},{24,19},{7,12},{15,20},{23,28}... | collective-permute-start | bytes 393224 | tf_op jit(solution)/shard_map/ppermute | solution.py:640
  5.7 4.5 %collective-permute-start.1 = (bf16[2,8,4096]{2,1,0:T(8,128)(2,1)S(1)}, bf16[2,8,4096]{2,1,0:T(8,128)(2,1)S(1)}, u32[]{:S(2)}, u32[]{:S(2)}) collective-permute-start(bf16[2,8,4096]{2,1,0:T(8,128)(2,1)S(1)} %get-tuple-element.16), channel_id=1, source_target_pairs={{1,2},{9,10},{17,18},{25,26},{2,1},{10,9},{18,17},{26,25},{5,6},{1... | collective-permute-start | bytes 393224 | tf_op jit(solution)/shard_map/ppermute | solution.py:640
  18.6 14.0 %collective-permute-start.3 = (f32[10,32,128]{2,1,0:T(8,128)S(1)}, f32[10,32,128]{2,1,0:T(8,128)S(1)}, u32[]{:S(2)}, u32[]{:S(2)}) collective-permute-start(f32[10,32,128]{2,1,0:T(8,128)S(1)} %get-tuple-element.25.numer), channel_id=1, source_target_pairs={{0,4},{4,0},{1,5},{5,1},{2,6},{6,2},{3,7},{7,3},{8,12},{12,8},{9,1... | collective-permute-start | bytes 491528 | tf_op jit(solution)/shard_map/ppermute | solution.py:668
where the time goes:
time: 34.5 us; the launch traced here: 34.3 us
  Pallas kernels  13.9 us (40%)
  blocking collectives  13.9 us (40%)
  starting transfers between devices  4.49 us (13%)
  local copies, waits for them, and re-layouts  1.2 us (3%)
  between operations  0.8 us (2%)
    all_to_all x1, blocking collectives, local(): lax.all_to_all(send, 'patch', split_axis=0, concat_axis=0, tiled=True)  13.9 us
    pallas_call x1, Pallas kernels, solve(): pl.pallas_call(functools.partial(solve_kernel, fibres, waves), out_shape=...  8.45 us
    ppermute x3, starting transfers between devices, exchange(): return lax.ppermute(value, axes, pairs + [(b, a) for a, b in pairs])  4.41 us
    pallas_call x1, Pallas kernels, prepare(): pl.pallas_call(prepare_kernel, out_shape=(made(rows, 2 * PC), made(PR, PC...  3.7 us
    pallas_call x1, Pallas kernels, finish(): pl.pallas_call(functools.partial(finish_kernel, capacity), out_shape=(jax...  1.65 us
    unnamed x16, local copies, waits for them, and re-layouts  1.2 us
  transfers between devices with their start and end apart: 4, of which 0 were waited for; matrix products, arithmetic and copies ran while one was open for 0% of the time, Pallas kernels for 11%

commit v1 on v0

--- a/solution.py
+++ b/solution.py
@@ -15,6 +15,8 @@
 SUB = 8
 HALF = LANES // 2
 CODE_BITS = 15.0
+CODE_WIDTH = 16
+CODE_MASK = 0xFFFF
 CODE_TOP = 32767.0
 TINY = 1e-30
 EDGE_FLOPS = 1 << 34
@@ -392,14 +394,11 @@
     image(1)
     move(0)
 
-    def turn_about(step, carry):
+    for _ in range(ITERS - 2):
         image(0)
         move(1)
         image(1)
         move(0)
-        return carry
-
-    lax.fori_loop(0, ITERS - 2, turn_about, 0)
     image(0, folded=False)
     move(1)
     image(1, folded=False)
@@ -439,13 +438,13 @@
                 ),
             )
             packed[target, pl.ds(slot * upper_rows, upper_rows), :] = compact
+    words = send.shape[1]
     for index in range(send.shape[0]):
-        send[index] = packed[index].astype(jnp.int32).astype(jnp.int16)
-
-
-def finish_kernel(
-    capacity, received, numer, others, spectra_out, coadd_out, spectra_ext, coadd, collected, sent
-):
+        codes = packed[index].astype(jnp.int32)
+        send[index] = (codes[:words] << CODE_WIDTH) | (codes[words:] & CODE_MASK)
+
+
+def coadd_kernel(numer, others, coadd, collected):
     fibres, patches, waves = coadd.shape
     padded_p = up(patches, SUB)
     lower_half = lax.broadcasted_iota(jnp.int32, numer.shape[1:], 1) < HALF
@@ -460,12 +459,17 @@
             collected[pl.ds(2 * pair + half, fibres, stride=padded_p), :] = value[:fibres]
     for f in range(fibres):
         coadd[f] = collected[f * padded_p : f * padded_p + patches, :waves]
-    copies = [pltpu.make_async_copy(coadd, coadd_out, sent.at[0])]
-    copies[0].start()
+
+
+def finish_kernel(capacity, received, spectra_ext):
+    _, fibres, _, waves = spectra_ext.shape
     upper_rows = (fibres + 1) // 2
-    lower_half = lax.broadcasted_iota(jnp.int32, received.shape[1:], 1) < HALF
+    coded_shape = (2 * received.shape[1], LANES)
+    lower_half = lax.broadcasted_iota(jnp.int32, coded_shape, 1) < HALF
     for source in range(received.shape[0]):
-        coded = received[source].astype(jnp.int32).astype(F32)
+        word = received[source]
+        codes = [word >> CODE_WIDTH, (word << CODE_WIDTH) >> CODE_WIDTH]
+        coded = jnp.concatenate(codes, axis=0).astype(F32)
         power = jnp.where(
             lower_half, coded[:, waves : waves + 1], coded[:, HALF + waves : HALF + waves + 1]
         )
@@ -477,14 +481,6 @@
             spectra_ext[entry, 0:upper_rows, 0, :] = value[at : at + upper_rows, :waves]
             at_end = at + fibres - upper_rows
             spectra_ext[entry, upper_rows:fibres, 0, :] = turned[at:at_end, :waves]
-        entries = pl.ds(source * capacity, capacity)
-        copy = pltpu.make_async_copy(
-            spectra_ext.at[entries], spectra_out.at[entries], sent.at[1 + source]
-        )
-        copy.start()
-        copies.append(copy)
-    for copy in copies:
-        copy.wait()
 
 
 def vmem(count=1):
@@ -545,7 +541,7 @@
     pairs = patches // 2
     main = fibres // SUB * SUB
     padded_f = up(fibres, SUB)
-    code_rows = up(capacity * ((fibres + 1) // 2), SUB)
+    code_rows = up(capacity * ((fibres + 1) // 2), 2 * SUB)
     vectors = pltpu.VMEM((pairs, padded_f, LANES), F32)
     sums = pltpu.VMEM((2, up((pairs + 1) // 2, SUB), LANES), F32)
     tops = pltpu.VMEM((patches, 2 * HALO, PC), BF16)
@@ -553,7 +549,7 @@
     return pl.pallas_call(
         functools.partial(solve_kernel, fibres, waves),
         out_shape=(
-            jax.ShapeDtypeStruct((group, code_rows, LANES), jnp.int16),
+            jax.ShapeDtypeStruct((group, code_rows // 2, LANES), jnp.int32),
             jax.ShapeDtypeStruct((pairs, padded_f, LANES), F32),
         ),
         in_specs=hbm(3) + vmem(10),
@@ -584,24 +580,29 @@
     )(row_off, col_off, dest, *halos, *prepared)
 
 
-def finish(received, numer, others, capacity, patches, fibres, waves):
+def frame_mean(numer, others, patches, fibres, waves):
+    return pl.pallas_call(
+        coadd_kernel,
+        out_shape=jax.ShapeDtypeStruct((fibres, patches, waves), F32),
+        in_specs=vmem(2),
+        out_specs=vmem()[0],
+        scratch_shapes=[pltpu.VMEM((fibres * up(patches, SUB), LANES), F32)],
+        cost_estimate=pl.CostEstimate(
+            flops=4 * numer.size, bytes_accessed=8 * numer.size, transcendentals=numer.size
+        ),
+        compiler_params=pltpu.CompilerParams(vmem_limit_bytes=16 * 1024 * 1024),
+    )(numer, others)
+
+
+def finish(received, capacity, fibres, waves):
     entries = received.shape[0] * capacity
     return pl.pallas_call(
         functools.partial(finish_kernel, capacity),
-        out_shape=(
-            jax.ShapeDtypeStruct((entries, fibres, 1, waves), F32),
-            jax.ShapeDtypeStruct((fibres, patches, waves), F32),
-        ),
-        in_specs=vmem(3),
-        out_specs=tuple(hbm(2)),
-        scratch_shapes=[
-            pltpu.VMEM((entries, fibres, 1, waves), F32),
-            pltpu.VMEM((fibres, patches, waves), F32),
-            pltpu.VMEM((fibres * up(patches, SUB), LANES), F32),
-            pltpu.SemaphoreType.DMA((1 + received.shape[0],)),
-        ],
+        out_shape=jax.ShapeDtypeStruct((entries, fibres, 1, waves), F32),
+        in_specs=vmem(1),
+        out_specs=vmem()[0],
         compiler_params=pltpu.CompilerParams(vmem_limit_bytes=16 * 1024 * 1024),
-    )(received, numer, others)
+    )(received)
 
 
 def edge_kernel(exposure, two, one):
@@ -669,7 +670,8 @@
             for hop in range(1, frames)
         ]
     )
-    spectra_ext, coadd = finish(received, numer, others, capacity, patches, fibres, waves)
+    coadd = frame_mean(numer, others, patches, fibres, waves)
+    spectra_ext = finish(received, capacity, fibres, waves)
     return spectra_ext.transpose(2, 0, 3, 1), coadd.transpose(1, 2, 0)
 
 

time: 34.5 us -> 34.4 us (level)
    pallas_call x1, Pallas kernels: 8.45 us -> 7.86 us  [solve(): pl.pallas_call(functools.partial(solve_kernel, fibres, waves), out_shape=...]
    pallas_call x1 -> x2, Pallas kernels: 1.65 us -> 2.14 us  [the longest x1 1.14 us: frame_mean(): pl.pallas_call(coadd_kernel, out_shape=jax.ShapeDtypeStruct((fibres, patc...]
  transfers between devices with their start and end apart: 4 -> 4, of which waited for: 0 -> 0; matrix products, arithmetic and copies ran while one was open for 0% -> 0% of each run, Pallas kernels for 11% -> 14%
where the time goes in v1:
time: 34.4 us; the launch traced here: 34.2 us
  blocking collectives  14 us (41%)
  Pallas kernels  13.8 us (40%)
  starting transfers between devices  4.49 us (13%)
  local copies, waits for them, and re-layouts  1.2 us (3%)
  between operations  0.8 us (2%)
    all_to_all x1, blocking collectives, local(): lax.all_to_all(send, 'patch', split_axis=0, concat_axis=0, tiled=True)  14 us
    pallas_call x1, Pallas kernels, solve(): pl.pallas_call(functools.partial(solve_kernel, fibres, waves), out_shape=...  7.86 us
    ppermute x3, starting transfers between devices, exchange(): return lax.ppermute(value, axes, pairs + [(b, a) for a, b in pairs])  4.41 us
    pallas_call x1, Pallas kernels, prepare(): pl.pallas_call(prepare_kernel, out_shape=(made(rows, 2 * PC), made(PR, PC...  3.7 us
    unnamed x16, local copies, waits for them, and re-layouts  1.2 us
    pallas_call x1, Pallas kernels, frame_mean(): pl.pallas_call(coadd_kernel, out_shape=jax.ShapeDtypeStruct((fibres, patc...  1.14 us
    pallas_call x1, Pallas kernels, finish(): pl.pallas_call(functools.partial(finish_kernel, capacity), out_shape=jax....  1.01 us
  transfers between devices with their start and end apart: 4, of which 0 were waited for; matrix products, arithmetic and copies ran while one was open for 0% of the time, Pallas kernels for 14%

profile of v1, /device:TPU:0, one launch (start us, length us, event | category | flops | bytes accessed | tf_op | source)
XLA Modules:
  0.0 34.2 jit_solution(9536950055206564597)
XLA Ops:
  0.6 0.0 copy-start
  0.6 1.2 %copy-done = bf16[1,2,56,4096]{3,2,1,0:T(8,128)(2,1)S(1)} copy-done((bf16[1,2,56,4096]{3,2,1,0:T(8,128)(2,1)S(1)}, bf16[1,2,56,4096]{3,2,1,0:T(8,128)(2,1)}, u32[]{:S(2)}) %copy-start) | copy-done | bytes 917528
  1.8 0.0 copy-start.5
  1.8 0.0 copy-start.6
  1.9 0.1 shard_map.86
  1.9 3.1 %collective-permute-start = (bf16[2,8,4096]{2,1,0:T(8,128)(2,1)S(1)}, bf16[2,8,4096]{2,1,0:T(8,128)(2,1)S(1)}, u32[]{:S(2)}, u32[]{:S(2)}) collective-permute-start(bf16[2,8,4096]{2,1,0:T(8,128)(2,1)S(1)} %get-tuple-element.13), channel_id=1, source_target_pairs={{0,1},{2,3},{8,9},{10,11},{16,17},{18,19},{24,25},{26,27},{1,0},{3... | collective-permute-start | bytes 393224 | tf_op jit(solution)/shard_map/ppermute | solution.py:641
  5.0 0.7 %collective-permute-start.2 = (bf16[2,8,4096]{2,1,0:T(8,128)(2,1)S(1)}, bf16[2,8,4096]{2,1,0:T(8,128)(2,1)S(1)}, u32[]{:S(2)}, u32[]{:S(2)}) collective-permute-start(bf16[2,8,4096]{2,1,0:T(8,128)(2,1)S(1)} %get-tuple-element.14), channel_id=1, source_target_pairs={{3,8},{11,16},{19,24},{8,3},{16,11},{24,19},{7,12},{15,20},{23,28}... | collective-permute-start | bytes 393224 | tf_op jit(solution)/shard_map/ppermute | solution.py:641
  5.7 0.7 %collective-permute-start.1 = (bf16[2,8,4096]{2,1,0:T(8,128)(2,1)S(1)}, bf16[2,8,4096]{2,1,0:T(8,128)(2,1)S(1)}, u32[]{:S(2)}, u32[]{:S(2)}) collective-permute-start(bf16[2,8,4096]{2,1,0:T(8,128)(2,1)S(1)} %get-tuple-element.14), channel_id=1, source_target_pairs={{1,2},{9,10},{17,18},{25,26},{2,1},{10,9},{18,17},{26,25},{5,6},{1... | collective-permute-start | bytes 393224 | tf_op jit(solution)/shard_map/ppermute | solution.py:641
  6.4 0.0 copy-done.1
  6.4 0.0 copy-done.2
  6.4 0.0 copy-done.3
  6.4 0.0 copy-done.4
  6.4 0.0 copy-done.5
  6.4 0.0 copy-done.6
  6.4 3.7 %shard_map.87 = (bf16[20,416,512]{2,1,0:T(8,128)(2,1)S(1)}, bf16[20,64,256]{2,1,0:T(8,128)(2,1)S(1)}, bf16[20,64,256]{2,1,0:T(8,128)(2,1)S(1)}, bf16[20,64,256]{...) custom-call(s32[20]{0:T(128)S(1)} %bitcast.20, ...), custom_call_target="tpu_custom_call" | custom-call | flops 17039360 | bytes 16777216 | tf_op jit(solution)/shard_map/pallas_call | solution.py:506
  10.1 0.0 collective-permute-done.halo_one
  10.1 0.0 collective-permute-done.2.halo_far
  10.2 0.0 collective-permute-done.1.halo_near
  10.2 7.9 %shard_map.88 = (s32[4,40,128]{2,1,0:T(8,128)S(1)}, f32[10,32,128]{2,1,0:T(8,128)S(1)}) custom-call(s32[20]{0:T(128)S(1)} %bitcast.21, s32[20]{0:T(128)S(1)} %bitcast.23, s32[20]{0:T(128)S(1)} %bitcast.24, bf16[2,8,4096]{2,1,0:T(8,128)(2,1)S(1)} %collective-permute-done.halo_one, bf16[2,8,4096]{2,1,0:T(8,128)(2,1)S(1)} %collective-permute-done.1.halo_near, ...), custom_call_target="tpu_custom_call" | custom-call | tf_op jit(solution)/shard_map/pallas_call | solution.py:549
  18.0 0.1 collective-permute-start.3
  18.1 14.0 %all_to_all.5.received = s32[4,40,128]{2,1,0:T(8,128)S(1)} all-to-all(s32[4,40,128]{2,1,0:T(8,128)S(1)} %get-tuple-element.22), channel_id=1, replica_groups=mesh['section'=4,'frame'=2,'patch'=4] {'patch'}, dimensions={0} | all-to-all | bytes 163840 | tf_op jit(solution)/shard_map/all_to_all | solution.py:666
  32.1 1.0 %shard_map.89 = f32[20,25,1,50]{3,2,1,0:T(1,128)} custom-call(s32[4,40,128]{2,1,0:T(8,128)S(1)} %all_to_all.5.received), custom_call_target="tpu_custom_call" | custom-call | tf_op jit(solution)/shard_map/pallas_call | solution.py:599
  33.1 0.0 collective-permute-done.3
  33.1 1.1 %shard_map.90 = f32[25,20,50]{2,1,0:T(8,128)} custom-call(f32[10,32,128]{2,1,0:T(8,128)S(1)} %get-tuple-element.23.numer, f32[1,10,32,128]{3,2,1,0:T(8,128)S(1)} %bitcast.18), custom_call_target="tpu_custom_call" | custom-call | flops 163840 | bytes 327680 | tf_op jit(solution)/shard_map/pallas_call | solution.py:584
  (6 shorter events, 0.0 us)
Async XLA Ops:
  0.6 1.2 %copy-start = (bf16[1,2,56,4096]{3,2,1,0:T(8,128)(2,1)S(1)}, bf16[1,2,56,4096]{3,2,1,0:T(8,128)(2,1)}, u32[]{:S(2)}) copy-start(bf16[1,2,56,4096]{3,2,1,0:T(8,128)(2,1)} %param.7) | copy-start | bytes 2752516
  1.8 4.6 %copy-start.1 = (bf16[1,2,56,4096]{3,2,1,0:T(8,128)(2,1)S(1)}, bf16[1,2,56,4096]{3,2,1,0:T(8,128)(2,1)}, u32[]{:S(2)}) copy-start(bf16[1,2,56,4096]{3,2,1,0:T(8,128)(2,1)} %param.7) | copy-start | bytes 2752516
  1.8 4.6 %copy-start.2 = (bf16[1,20,25,256]{3,1,2,0:T(8,128)(2,1)S(1)}, bf16[1,20,25,256]{3,1,2,0:T(8,128)(2,1)}, u32[]{:S(2)}) copy-start(bf16[1,20,25,256]{3,1,2,0:T(8,128)(2,1)} %param.9) | copy-start | bytes 768004
  1.8 4.6 %copy-start.3 = (bf16[1,20,50,64]{3,2,1,0:T(8,128)(2,1)S(1)}, bf16[1,20,50,64]{3,2,1,0:T(8,128)(2,1)}, u32[]{:S(2)}) copy-start(bf16[1,20,50,64]{3,2,1,0:T(8,128)(2,1)} %param.8) | copy-start | bytes 384004
  1.8 4.6 %copy-start.4 = (f32[1,20,25]{2,0,1:T(1,128)S(1)}, f32[1,20,25]{2,0,1:T(1,128)}, u32[]{:S(2)}) copy-start(f32[1,20,25]{2,0,1:T(1,128)} %param.13) | copy-start | bytes 6004
  1.8 4.6 %copy-start.5 = (s32[1,20]{1,0:T(1,128)S(1)}, s32[1,20]{1,0:T(1,128)}, u32[]{:S(2)}) copy-start(s32[1,20]{1,0:T(1,128)} %param.10) | copy-start | bytes 244
  1.8 4.6 %copy-start.6 = (s32[1,20]{1,0:T(1,128)S(1)}, s32[1,20]{1,0:T(1,128)}, u32[]{:S(2)}) copy-start(s32[1,20]{1,0:T(1,128)} %param.11) | copy-start | bytes 244
  1.8 8.3 %copy-start.7 = (s32[1,20]{1,0:T(1,128)S(1)}, s32[1,20]{1,0:T(1,128)}, u32[]{:S(2)}) copy-start(s32[1,20]{1,0:T(1,128)} %param.12) | copy-start | bytes 244
  1.9 8.2 %collective-permute-start = (bf16[2,8,4096]{2,1,0:T(8,128)(2,1)S(1)}, bf16[2,8,4096]{2,1,0:T(8,128)(2,1)S(1)}, u32[]{:S(2)}, u32[]{:S(2)}) collective-permute-start(bf16[2,8,4096]{2,1,0:T(8,128)(2,1)S(1)} %get-tuple-element.13), channel_id=1, source_target_pairs={{0,1},{2,3},{8,9},{10,11},{16,17},{18,19},{24,25},{26,27},{1,0},{3... | collective-permute-start | bytes 393224 | tf_op jit(solution)/shard_map/ppermute | solution.py:641
  5.0 5.1 %collective-permute-start.2 = (bf16[2,8,4096]{2,1,0:T(8,128)(2,1)S(1)}, bf16[2,8,4096]{2,1,0:T(8,128)(2,1)S(1)}, u32[]{:S(2)}, u32[]{:S(2)}) collective-permute-start(bf16[2,8,4096]{2,1,0:T(8,128)(2,1)S(1)} %get-tuple-element.14), channel_id=1, source_target_pairs={{3,8},{11,16},{19,24},{8,3},{16,11},{24,19},{7,12},{15,20},{23,28}... | collective-permute-start | bytes 393224 | tf_op jit(solution)/shard_map/ppermute | solution.py:641
  5.7 4.5 %collective-permute-start.1 = (bf16[2,8,4096]{2,1,0:T(8,128)(2,1)S(1)}, bf16[2,8,4096]{2,1,0:T(8,128)(2,1)S(1)}, u32[]{:S(2)}, u32[]{:S(2)}) collective-permute-start(bf16[2,8,4096]{2,1,0:T(8,128)(2,1)S(1)} %get-tuple-element.14), channel_id=1, source_target_pairs={{1,2},{9,10},{17,18},{25,26},{2,1},{10,9},{18,17},{26,25},{5,6},{1... | collective-permute-start | bytes 393224 | tf_op jit(solution)/shard_map/ppermute | solution.py:641
  18.0 15.0 %collective-permute-start.3 = (f32[10,32,128]{2,1,0:T(8,128)S(1)}, f32[10,32,128]{2,1,0:T(8,128)S(1)}, u32[]{:S(2)}, u32[]{:S(2)}) collective-permute-start(f32[10,32,128]{2,1,0:T(8,128)S(1)} %get-tuple-element.23.numer), channel_id=1, source_target_pairs={{0,4},{4,0},{1,5},{5,1},{2,6},{6,2},{3,7},{7,3},{8,12},{12,8},{9,1... | collective-permute-start | bytes 491528 | tf_op jit(solution)/shard_map/ppermute | solution.py:669

commit v2 on v0

--- a/solution.py
+++ b/solution.py
@@ -203,6 +203,7 @@
     norm,
     packed,
     counts,
+    slots,
     arrived,
 ):
     copies = start_copies(
@@ -235,7 +236,7 @@
     def beside_own(edge, own):
         return jnp.concatenate([edge, own.astype(F32)[HALO:]], axis=0).astype(BF16)
 
-    for patch in range(patches):
+    def cut_halo(patch):
         first_row = row_off[patch]
         first_col = col_off[patch]
         base = first_col // LANES
@@ -276,23 +277,29 @@
             axis=0,
         )
 
-    for pair in range(pairs):
-        one, two = 2 * pair, 2 * pair + 1
-        folded = dot_nt(
-            jnp.concatenate([fibre[one], fibre[one], fibre[two], fibre[two]], axis=1),
-            diagonal(
-                [whole(top_upper, upper_wx, one), whole(top_lower, lower_wx, one)],
-                [whole(top_upper, upper_wx, two), whole(top_lower, lower_wx, two)],
-            ),
-        )
-        imaged[pair] = folded
-    for pair in range(pairs):
-        rhs = two_pass(dot_nt, imaged[pair], row_block[pair])
-        residual[pair] = rhs
-        direction[pair] = rhs
-        estimate[pair] = jnp.zeros_like(rhs)
-        set_partial(pair, jnp.sum(rhs * rhs, axis=0, keepdims=True))
-    for pair in range(pairs):
+    def begin(half):
+        some = members[half]
+        for pair in some:
+            cut_halo(2 * pair)
+            cut_halo(2 * pair + 1)
+        for pair in some:
+            one, two = 2 * pair, 2 * pair + 1
+            imaged[pair] = dot_nt(
+                jnp.concatenate([fibre[one], fibre[one], fibre[two], fibre[two]], axis=1),
+                diagonal(
+                    [whole(top_upper, upper_wx, one), whole(top_lower, lower_wx, one)],
+                    [whole(top_upper, upper_wx, two), whole(top_lower, lower_wx, two)],
+                ),
+            )
+        for pair in some:
+            rhs = two_pass(dot_nt, imaged[pair], row_block[pair])
+            residual[pair] = rhs
+            direction[pair] = rhs
+            estimate[pair] = jnp.zeros_like(rhs)
+            set_partial(pair, jnp.sum(rhs * rhs, axis=0, keepdims=True))
+        norm[half] = patch_sums(partial[half])
+
+    def build(pair):
         one, two = 2 * pair, 2 * pair + 1
         blended = dot_nt(
             jnp.concatenate([products[one], products[two]], axis=1),
@@ -354,9 +361,13 @@
             imaged[pair, main:padded_f, :] = rest
         set_partial(pair, product)
 
-    def image(half, folded=True):
+    def image(half, folded=True, beside=()):
         some = [members[half][at : at + 2] for at in range(0, len(members[half]), 2)]
-        for turn in range(len(some) + 2):
+        turns = len(some) + 2
+        share = -(-len(beside) // turns)
+        for turn in range(turns):
+            for work in beside[turn * share : (turn + 1) * share]:
+                work()
             if turn < len(some):
                 apply(dot_nn, direction, across, some[turn])
             if 0 <= turn - 1 < len(some):
@@ -386,35 +397,21 @@
             direction[pair] = residual[pair] + ratio[row : row + 1] * direction[pair]
         norm[half] = norm_next
 
-    for half in range(halves):
-        norm[half] = patch_sums(partial[half])
-    image(0)
-    image(1)
-    move(0)
-
-    def turn_about(step, carry):
-        image(0)
-        move(1)
-        image(1)
-        move(0)
-        return carry
-
-    lax.fori_loop(0, ITERS - 2, turn_about, 0)
-    image(0, folded=False)
-    move(1)
-    image(1, folded=False)
-    advance(0)
-    advance(1)
-
     copies[2].wait()
     for index in range(send.shape[0]):
         counts[index] = 0
+    for patch in range(patches):
+        target = dest[patch]
+        slot = counts[target]
+        counts[target] = slot + 1
+        slots[patch] = slot
     packed[...] = jnp.zeros_like(packed)
     upper_rows = (fibres + 1) // 2
     lane_f = lax.broadcasted_iota(jnp.int32, (padded_f, LANES), 1)
     at_wave = lax.rem(lane_f, HALF) == waves
     unit = jnp.where(at_wave, 1.0, 0.0)
-    for pair in range(pairs):
+
+    def hand_over(pair):
         spectra = estimate[pair]
         numer[pair] = (spectra + unit) * (weight_lanes[2 * pair] + weight_lanes[2 * pair + 1])
         size = jnp.abs(spectra)
@@ -428,9 +425,6 @@
         for half in range(2):
             here = turned if half else coded
             away = coded if half else turned
-            target = dest[2 * pair + half]
-            slot = counts[target]
-            counts[target] = slot + 1
             compact = jnp.where(
                 lane_f[:upper_rows] < HALF,
                 here[:upper_rows],
@@ -438,7 +432,28 @@
                     [away[upper_rows:fibres], away[: 2 * upper_rows - fibres]], axis=0
                 ),
             )
-            packed[target, pl.ds(slot * upper_rows, upper_rows), :] = compact
+            rows = pl.ds(slots[2 * pair + half] * upper_rows, upper_rows)
+            packed[dest[2 * pair + half], rows, :] = compact
+
+    begin(0)
+    for pair in members[0]:
+        build(pair)
+    begin(1)
+    image(0, beside=[functools.partial(build, pair) for pair in members[1]])
+    image(1)
+    move(0)
+    for _ in range(ITERS - 2):
+        image(0)
+        move(1)
+        image(1)
+        move(0)
+    image(0, folded=False)
+    move(1)
+    advance(0)
+    image(1, folded=False, beside=[functools.partial(hand_over, pair) for pair in members[0]])
+    advance(1)
+    for pair in members[1]:
+        hand_over(pair)
     for index in range(send.shape[0]):
         send[index] = packed[index].astype(jnp.int32).astype(jnp.int16)
 
@@ -578,6 +593,7 @@
             sums,
             pltpu.VMEM((group, code_rows, LANES), F32),
             pltpu.SMEM((group,), jnp.int32),
+            pltpu.SMEM((patches,), jnp.int32),
             pltpu.SemaphoreType.DMA((3,)),
         ],
         compiler_params=pltpu.CompilerParams(vmem_limit_bytes=24 * 1024 * 1024),

time: 34.5 us -> 33.5 us (0.971)
  Pallas kernels: 13.9 us -> 12.9 us
    pallas_call x1, Pallas kernels: 8.45 us -> 7.43 us  [solve(): pl.pallas_call(functools.partial(solve_kernel, fibres, waves), out_shape=...]
where the time goes in v2:
time: 33.5 us; the launch traced here: 33.3 us
  blocking collectives  13.9 us (41%)
  Pallas kernels  12.9 us (39%)
  starting transfers between devices  4.49 us (13%)
  local copies, waits for them, and re-layouts  1.2 us (4%)
  between operations  0.8 us (2%)
    all_to_all x1, blocking collectives, local(): lax.all_to_all(send, 'patch', split_axis=0, concat_axis=0, tiled=True)  13.9 us
    pallas_call x1, Pallas kernels, solve(): pl.pallas_call(functools.partial(solve_kernel, fibres, waves), out_shape=...  7.43 us
    ppermute x3, starting transfers between devices, exchange(): return lax.ppermute(value, axes, pairs + [(b, a) for a, b in pairs])  4.41 us
    pallas_call x1, Pallas kernels, prepare(): pl.pallas_call(prepare_kernel, out_shape=(made(rows, 2 * PC), made(PR, PC...  3.7 us
    pallas_call x1, Pallas kernels, finish(): pl.pallas_call(functools.partial(finish_kernel, capacity), out_shape=(jax...  1.65 us
    unnamed x16, local copies, waits for them, and re-layouts  1.2 us
  transfers between devices with their start and end apart: 4, of which 0 were waited for; matrix products, arithmetic and copies ran while one was open for 0% of the time, Pallas kernels for 11%

profile of v2, /device:TPU:0, one launch (start us, length us, event | category | flops | bytes accessed | tf_op | source)
XLA Modules:
  0.0 33.3 jit_solution(5297572675523464399)
XLA Ops:
  0.6 0.0 copy-start
  0.6 1.2 %copy-done = bf16[1,2,56,4096]{3,2,1,0:T(8,128)(2,1)S(1)} copy-done((bf16[1,2,56,4096]{3,2,1,0:T(8,128)(2,1)S(1)}, bf16[1,2,56,4096]{3,2,1,0:T(8,128)(2,1)}, u32[]{:S(2)}) %copy-start) | copy-done | bytes 917528
  1.8 0.0 copy-start.5
  1.8 0.0 copy-start.6
  1.8 0.0 copy-start.7
  1.9 0.1 shard_map.86
  1.9 3.1 %collective-permute-start = (bf16[2,8,4096]{2,1,0:T(8,128)(2,1)S(1)}, bf16[2,8,4096]{2,1,0:T(8,128)(2,1)S(1)}, u32[]{:S(2)}, u32[]{:S(2)}) collective-permute-start(bf16[2,8,4096]{2,1,0:T(8,128)(2,1)S(1)} %get-tuple-element.15), channel_id=1, source_target_pairs={{0,1},{2,3},{8,9},{10,11},{16,17},{18,19},{24,25},{26,27},{1,0},{3... | collective-permute-start | bytes 393224 | tf_op jit(solution)/shard_map/ppermute | solution.py:656
  5.0 0.7 %collective-permute-start.2 = (bf16[2,8,4096]{2,1,0:T(8,128)(2,1)S(1)}, bf16[2,8,4096]{2,1,0:T(8,128)(2,1)S(1)}, u32[]{:S(2)}, u32[]{:S(2)}) collective-permute-start(bf16[2,8,4096]{2,1,0:T(8,128)(2,1)S(1)} %get-tuple-element.16), channel_id=1, source_target_pairs={{3,8},{11,16},{19,24},{8,3},{16,11},{24,19},{7,12},{15,20},{23,28}... | collective-permute-start | bytes 393224 | tf_op jit(solution)/shard_map/ppermute | solution.py:656
  5.7 0.7 %collective-permute-start.1 = (bf16[2,8,4096]{2,1,0:T(8,128)(2,1)S(1)}, bf16[2,8,4096]{2,1,0:T(8,128)(2,1)S(1)}, u32[]{:S(2)}, u32[]{:S(2)}) collective-permute-start(bf16[2,8,4096]{2,1,0:T(8,128)(2,1)S(1)} %get-tuple-element.16), channel_id=1, source_target_pairs={{1,2},{9,10},{17,18},{25,26},{2,1},{10,9},{18,17},{26,25},{5,6},{1... | collective-permute-start | bytes 393224 | tf_op jit(solution)/shard_map/ppermute | solution.py:656
  6.4 0.0 copy-done.1
  6.4 0.0 copy-done.2
  6.4 0.0 copy-done.3
  6.4 0.0 copy-done.4
  6.4 0.0 copy-done.5
  6.4 0.0 copy-done.6
  6.4 3.7 %shard_map.87 = (bf16[20,416,512]{2,1,0:T(8,128)(2,1)S(1)}, bf16[20,64,256]{2,1,0:T(8,128)(2,1)S(1)}, bf16[20,64,256]{2,1,0:T(8,128)(2,1)S(1)}, bf16[20,64,256]{...) custom-call(s32[20]{0:T(128)S(1)} %bitcast.20, ...), custom_call_target="tpu_custom_call" | custom-call | flops 17039360 | bytes 16777216 | tf_op jit(solution)/shard_map/pallas_call | solution.py:525
  10.1 0.0 collective-permute-done.halo_one
  10.1 0.0 collective-permute-done.2.halo_far
  10.2 0.0 collective-permute-done.1.halo_near
  10.2 7.4 %shard_map.88 = (s16[4,72,128]{2,1,0:T(8,128)(2,1)S(1)}, f32[10,32,128]{2,1,0:T(8,128)S(1)}) custom-call(s32[20]{0:T(128)S(1)} %bitcast.21, s32[20]{0:T(128)S(1)} %bitcast.23, s32[20]{0:T(128)S(1)} %bitcast.24, bf16[2,8,4096]{2,1,0:T(8,128)(2,1)S(1)} %collective-permute-done.halo_one, bf16[2,8,4096]{2,1,0:T(8,128)(2,1)S(1)} %collective-permute-done.1.halo_near, ...), custom_call_target="tpu_custom_call" | custom-call | tf_op jit(solution)/shard_map/pallas_call | solution.py:568
  17.6 0.1 collective-permute-start.3
  17.7 13.9 %all_to_all.5.received = s16[4,72,128]{2,1,0:T(8,128)(2,1)S(1)} all-to-all(s16[4,72,128]{2,1,0:T(8,128)(2,1)S(1)} %get-tuple-element.24), channel_id=1, replica_groups=mesh['section'=4,'frame'=2,'patch'=4] {'patch'}, dimensions={0} | all-to-all | bytes 147456 | tf_op jit(solution)/shard_map/all_to_all | solution.py:681
  31.6 0.0 collective-permute-done.3
  31.6 1.6 %shard_map.89 = (f32[20,25,1,50]{3,2,1,0:T(1,128)}, f32[25,20,50]{2,1,0:T(8,128)}) custom-call(s16[4,72,128]{2,1,0:T(8,128)(2,1)S(1)} %all_to_all.5.received, f32[10,32,128]{2,1,0:T(8,128)S(1)} %get-tuple-element.25.numer, f32[1,10,32,128]{3,2,1,0:T(8,128)S(1)} %bitcast.18), custom_call_target="tpu_custom_call" | custom-call | tf_op jit(solution)/shard_map/pallas_call | solution.py:605
  (5 shorter events, 0.0 us)
Async XLA Ops:
  0.6 1.2 %copy-start = (bf16[1,2,56,4096]{3,2,1,0:T(8,128)(2,1)S(1)}, bf16[1,2,56,4096]{3,2,1,0:T(8,128)(2,1)}, u32[]{:S(2)}) copy-start(bf16[1,2,56,4096]{3,2,1,0:T(8,128)(2,1)} %param.7) | copy-start | bytes 2752516
  1.8 4.6 %copy-start.1 = (bf16[1,2,56,4096]{3,2,1,0:T(8,128)(2,1)S(1)}, bf16[1,2,56,4096]{3,2,1,0:T(8,128)(2,1)}, u32[]{:S(2)}) copy-start(bf16[1,2,56,4096]{3,2,1,0:T(8,128)(2,1)} %param.7) | copy-start | bytes 2752516
  1.8 4.6 %copy-start.2 = (bf16[1,20,25,256]{3,1,2,0:T(8,128)(2,1)S(1)}, bf16[1,20,25,256]{3,1,2,0:T(8,128)(2,1)}, u32[]{:S(2)}) copy-start(bf16[1,20,25,256]{3,1,2,0:T(8,128)(2,1)} %param.9) | copy-start | bytes 768004
  1.8 4.6 %copy-start.3 = (bf16[1,20,50,64]{3,2,1,0:T(8,128)(2,1)S(1)}, bf16[1,20,50,64]{3,2,1,0:T(8,128)(2,1)}, u32[]{:S(2)}) copy-start(bf16[1,20,50,64]{3,2,1,0:T(8,128)(2,1)} %param.8) | copy-start | bytes 384004
  1.8 4.6 %copy-start.4 = (f32[1,20,25]{2,0,1:T(1,128)S(1)}, f32[1,20,25]{2,0,1:T(1,128)}, u32[]{:S(2)}) copy-start(f32[1,20,25]{2,0,1:T(1,128)} %param.13) | copy-start | bytes 6004
  1.8 4.6 %copy-start.5 = (s32[1,20]{1,0:T(1,128)S(1)}, s32[1,20]{1,0:T(1,128)}, u32[]{:S(2)}) copy-start(s32[1,20]{1,0:T(1,128)} %param.10) | copy-start | bytes 244
  1.8 4.6 %copy-start.6 = (s32[1,20]{1,0:T(1,128)S(1)}, s32[1,20]{1,0:T(1,128)}, u32[]{:S(2)}) copy-start(s32[1,20]{1,0:T(1,128)} %param.11) | copy-start | bytes 244
  1.8 8.3 %copy-start.7 = (s32[1,20]{1,0:T(1,128)S(1)}, s32[1,20]{1,0:T(1,128)}, u32[]{:S(2)}) copy-start(s32[1,20]{1,0:T(1,128)} %param.12) | copy-start | bytes 244
  1.9 8.2 %collective-permute-start = (bf16[2,8,4096]{2,1,0:T(8,128)(2,1)S(1)}, bf16[2,8,4096]{2,1,0:T(8,128)(2,1)S(1)}, u32[]{:S(2)}, u32[]{:S(2)}) collective-permute-start(bf16[2,8,4096]{2,1,0:T(8,128)(2,1)S(1)} %get-tuple-element.15), channel_id=1, source_target_pairs={{0,1},{2,3},{8,9},{10,11},{16,17},{18,19},{24,25},{26,27},{1,0},{3... | collective-permute-start | bytes 393224 | tf_op jit(solution)/shard_map/ppermute | solution.py:656
  5.0 5.1 %collective-permute-start.2 = (bf16[2,8,4096]{2,1,0:T(8,128)(2,1)S(1)}, bf16[2,8,4096]{2,1,0:T(8,128)(2,1)S(1)}, u32[]{:S(2)}, u32[]{:S(2)}) collective-permute-start(bf16[2,8,4096]{2,1,0:T(8,128)(2,1)S(1)} %get-tuple-element.16), channel_id=1, source_target_pairs={{3,8},{11,16},{19,24},{8,3},{16,11},{24,19},{7,12},{15,20},{23,28}... | collective-permute-start | bytes 393224 | tf_op jit(solution)/shard_map/ppermute | solution.py:656
  5.7 4.5 %collective-permute-start.1 = (bf16[2,8,4096]{2,1,0:T(8,128)(2,1)S(1)}, bf16[2,8,4096]{2,1,0:T(8,128)(2,1)S(1)}, u32[]{:S(2)}, u32[]{:S(2)}) collective-permute-start(bf16[2,8,4096]{2,1,0:T(8,128)(2,1)S(1)} %get-tuple-element.16), channel_id=1, source_target_pairs={{1,2},{9,10},{17,18},{25,26},{2,1},{10,9},{18,17},{26,25},{5,6},{1... | collective-permute-start | bytes 393224 | tf_op jit(solution)/shard_map/ppermute | solution.py:656
  17.6 14.0 %collective-permute-start.3 = (f32[10,32,128]{2,1,0:T(8,128)S(1)}, f32[10,32,128]{2,1,0:T(8,128)S(1)}, u32[]{:S(2)}, u32[]{:S(2)}) collective-permute-start(f32[10,32,128]{2,1,0:T(8,128)S(1)} %get-tuple-element.25.numer), channel_id=1, source_target_pairs={{0,4},{4,0},{1,5},{5,1},{2,6},{6,2},{3,7},{7,3},{8,12},{12,8},{9,1... | collective-permute-start | bytes 491528 | tf_op jit(solution)/shard_map/ppermute | solution.py:684

commit v3 on v2

--- a/solution.py
+++ b/solution.py
@@ -214,6 +214,7 @@
     blocks = fibres // SUB
     main = blocks * SUB
     padded_f = up(fibres, SUB)
+    padded_p = up(patches, SUB)
     tiles = block_tiles(fibres)
     rank = lax.axis_index("section") * lax.axis_size("patch") + lax.axis_index("patch")
     odd = lax.rem(rank, 2) == 1
@@ -258,12 +259,13 @@
         top_upper[patch] = beside_own(above, upper_wx[patch, : 2 * HALO, :])
         top_lower[patch] = beside_own(edges[1] - above, lower_wx[patch, : 2 * HALO, :])
 
-    halves = partial.shape[0]
-    members = [list(range(at, pairs, halves)) for at in range(halves)]
+    fewer = pairs // 4 * 2
+    members = [list(range(fewer)), list(range(fewer, pairs))]
 
     def set_partial(pair, value):
-        row = pair // halves
-        partial[pair % halves, row : row + 1, :] = value
+        half = int(pair >= fewer)
+        row = members[half].index(pair)
+        partial[half, row : row + 1, :] = value
 
     def whole(top, own, patch):
         return jnp.concatenate([top[patch], own[patch, 2 * HALO :, :]], axis=0)
@@ -406,6 +408,7 @@
         counts[target] = slot + 1
         slots[patch] = slot
     packed[...] = jnp.zeros_like(packed)
+    numer[...] = jnp.zeros_like(numer)
     upper_rows = (fibres + 1) // 2
     lane_f = lax.broadcasted_iota(jnp.int32, (padded_f, LANES), 1)
     at_wave = lax.rem(lane_f, HALF) == waves
@@ -413,7 +416,10 @@
 
     def hand_over(pair):
         spectra = estimate[pair]
-        numer[pair] = (spectra + unit) * (weight_lanes[2 * pair] + weight_lanes[2 * pair + 1])
+        weighted = (spectra + unit) * (weight_lanes[2 * pair] + weight_lanes[2 * pair + 1])
+        for half in range(2):
+            value = pltpu.roll(weighted, HALF, 1) if half else weighted
+            numer[pl.ds(2 * pair + half, fibres, stride=padded_p), :] = value[:fibres]
         size = jnp.abs(spectra)
         first = jnp.max(jnp.where(lane_f < HALF, size, 0.0), axis=1, keepdims=True)
         second = jnp.max(jnp.where(lane_f < HALF, 0.0, size), axis=1, keepdims=True)
@@ -458,25 +464,16 @@
         send[index] = packed[index].astype(jnp.int32).astype(jnp.int16)
 
 
-def finish_kernel(
-    capacity, received, numer, others, spectra_out, coadd_out, spectra_ext, coadd, collected, sent
-):
+def finish_kernel(capacity, received, numer, others, spectra_ext, coadd):
     fibres, patches, waves = coadd.shape
     padded_p = up(patches, SUB)
-    lower_half = lax.broadcasted_iota(jnp.int32, numer.shape[1:], 1) < HALF
-    for pair in range(numer.shape[0]):
-        total = numer[pair]
+    for f in range(fibres):
+        rows = slice(f * padded_p, (f + 1) * padded_p)
+        total = numer[rows, :]
         for index in range(others.shape[0]):
-            total = total + others[index, pair]
-        first, second = total[:, waves : waves + 1], total[:, HALF + waves : HALF + waves + 1]
-        mean = total / jnp.where(lower_half, first, second)
-        for half in range(2):
-            value = pltpu.roll(mean, HALF, 1) if half else mean
-            collected[pl.ds(2 * pair + half, fibres, stride=padded_p), :] = value[:fibres]
-    for f in range(fibres):
-        coadd[f] = collected[f * padded_p : f * padded_p + patches, :waves]
-    copies = [pltpu.make_async_copy(coadd, coadd_out, sent.at[0])]
-    copies[0].start()
+            total = total + others[index, rows, :]
+        total = total[:patches]
+        coadd[f] = total[:, :waves] / total[:, waves : waves + 1]
     upper_rows = (fibres + 1) // 2
     lower_half = lax.broadcasted_iota(jnp.int32, received.shape[1:], 1) < HALF
     for source in range(received.shape[0]):
@@ -492,14 +489,6 @@
             spectra_ext[entry, 0:upper_rows, 0, :] = value[at : at + upper_rows, :waves]
             at_end = at + fibres - upper_rows
             spectra_ext[entry, upper_rows:fibres, 0, :] = turned[at:at_end, :waves]
-        entries = pl.ds(source * capacity, capacity)
-        copy = pltpu.make_async_copy(
-            spectra_ext.at[entries], spectra_out.at[entries], sent.at[1 + source]
-        )
-        copy.start()
-        copies.append(copy)
-    for copy in copies:
-        copy.wait()
 
 
 def vmem(count=1):
@@ -562,14 +551,14 @@
     padded_f = up(fibres, SUB)
     code_rows = up(capacity * ((fibres + 1) // 2), SUB)
     vectors = pltpu.VMEM((pairs, padded_f, LANES), F32)
-    sums = pltpu.VMEM((2, up((pairs + 1) // 2, SUB), LANES), F32)
+    sums = pltpu.VMEM((2, up(pairs - pairs // 4 * 2, SUB), LANES), F32)
     tops = pltpu.VMEM((patches, 2 * HALO, PC), BF16)
     halo_band = pltpu.VMEM((columns // LANES + 1, 2 * HALO, LANES), F32)
     return pl.pallas_call(
         functools.partial(solve_kernel, fibres, waves),
         out_shape=(
             jax.ShapeDtypeStruct((group, code_rows, LANES), jnp.int16),
-            jax.ShapeDtypeStruct((pairs, padded_f, LANES), F32),
+            jax.ShapeDtypeStruct((fibres * up(patches, SUB), LANES), F32),
         ),
         in_specs=hbm(3) + vmem(10),
         out_specs=tuple(vmem(2)),
@@ -609,13 +598,7 @@
             jax.ShapeDtypeStruct((fibres, patches, waves), F32),
         ),
         in_specs=vmem(3),
-        out_specs=tuple(hbm(2)),
-        scratch_shapes=[
-            pltpu.VMEM((entries, fibres, 1, waves), F32),
-            pltpu.VMEM((fibres, patches, waves), F32),
-            pltpu.VMEM((fibres * up(patches, SUB), LANES), F32),
-            pltpu.SemaphoreType.DMA((1 + received.shape[0],)),
-        ],
+        out_specs=tuple(vmem(2)),
         compiler_params=pltpu.CompilerParams(vmem_limit_bytes=16 * 1024 * 1024),
     )(received, numer, others)
 

time: 33.5 us -> 33.2 us (level)
  Pallas kernels: 12.9 us -> 12.5 us
    pallas_call x1, Pallas kernels: 1.65 us -> 1.19 us  [finish(): pl.pallas_call(functools.partial(finish_kernel, capacity), out_shape=(jax...]
where the time goes in v3:
time: 33.2 us; the launch traced here: 32.9 us
  blocking collectives  13.9 us (42%)
  Pallas kernels  12.5 us (38%)
  starting transfers between devices  4.49 us (14%)
  local copies, waits for them, and re-layouts  1.2 us (4%)
  between operations  0.8 us (2%)
    all_to_all x1, blocking collectives, local(): lax.all_to_all(send, 'patch', split_axis=0, concat_axis=0, tiled=True)  13.9 us
    pallas_call x1, Pallas kernels, solve(): pl.pallas_call(functools.partial(solve_kernel, fibres, waves), out_shape=...  7.55 us
    ppermute x3, starting transfers between devices, exchange(): return lax.ppermute(value, axes, pairs + [(b, a) for a, b in pairs])  4.41 us
    pallas_call x1, Pallas kernels, prepare(): pl.pallas_call(prepare_kernel, out_shape=(made(rows, 2 * PC), made(PR, PC...  3.7 us
    unnamed x16, local copies, waits for them, and re-layouts  1.2 us
    pallas_call x1, Pallas kernels, finish(): pl.pallas_call(functools.partial(finish_kernel, capacity), out_shape=(jax...  1.19 us
  transfers between devices with their start and end apart: 4, of which 0 were waited for; matrix products, arithmetic and copies ran while one was open for 0% of the time, Pallas kernels for 11%

profile of v3, /device:TPU:0, one launch (start us, length us, event | category | flops | bytes accessed | tf_op | source)
XLA Modules:
  0.0 32.9 jit_solution(13874979490991331449)
XLA Ops:
  0.6 0.0 copy-start
  0.6 1.2 %copy-done = bf16[1,2,56,4096]{3,2,1,0:T(8,128)(2,1)S(1)} copy-done((bf16[1,2,56,4096]{3,2,1,0:T(8,128)(2,1)S(1)}, bf16[1,2,56,4096]{3,2,1,0:T(8,128)(2,1)}, u32[]{:S(2)}) %copy-start) | copy-done | bytes 917528
  1.8 0.0 copy-start.5
  1.8 0.0 copy-start.6
  1.8 0.0 copy-start.7
  1.9 0.1 shard_map.86
  1.9 3.1 %collective-permute-start = (bf16[2,8,4096]{2,1,0:T(8,128)(2,1)S(1)}, bf16[2,8,4096]{2,1,0:T(8,128)(2,1)S(1)}, u32[]{:S(2)}, u32[]{:S(2)}) collective-permute-start(bf16[2,8,4096]{2,1,0:T(8,128)(2,1)S(1)} %get-tuple-element.15), channel_id=1, source_target_pairs={{0,1},{2,3},{8,9},{10,11},{16,17},{18,19},{24,25},{26,27},{1,0},{3... | collective-permute-start | bytes 393224 | tf_op jit(solution)/shard_map/ppermute | solution.py:639
  5.0 0.7 %collective-permute-start.2 = (bf16[2,8,4096]{2,1,0:T(8,128)(2,1)S(1)}, bf16[2,8,4096]{2,1,0:T(8,128)(2,1)S(1)}, u32[]{:S(2)}, u32[]{:S(2)}) collective-permute-start(bf16[2,8,4096]{2,1,0:T(8,128)(2,1)S(1)} %get-tuple-element.16), channel_id=1, source_target_pairs={{3,8},{11,16},{19,24},{8,3},{16,11},{24,19},{7,12},{15,20},{23,28}... | collective-permute-start | bytes 393224 | tf_op jit(solution)/shard_map/ppermute | solution.py:639
  5.7 0.7 %collective-permute-start.1 = (bf16[2,8,4096]{2,1,0:T(8,128)(2,1)S(1)}, bf16[2,8,4096]{2,1,0:T(8,128)(2,1)S(1)}, u32[]{:S(2)}, u32[]{:S(2)}) collective-permute-start(bf16[2,8,4096]{2,1,0:T(8,128)(2,1)S(1)} %get-tuple-element.16), channel_id=1, source_target_pairs={{1,2},{9,10},{17,18},{25,26},{2,1},{10,9},{18,17},{26,25},{5,6},{1... | collective-permute-start | bytes 393224 | tf_op jit(solution)/shard_map/ppermute | solution.py:639
  6.4 0.0 copy-done.1
  6.4 0.0 copy-done.2
  6.4 0.0 copy-done.3
  6.4 0.0 copy-done.4
  6.4 0.0 copy-done.5
  6.4 3.7 %shard_map.87 = (bf16[20,416,512]{2,1,0:T(8,128)(2,1)S(1)}, bf16[20,64,256]{2,1,0:T(8,128)(2,1)S(1)}, bf16[20,64,256]{2,1,0:T(8,128)(2,1)S(1)}, bf16[20,64,256]{...) custom-call(s32[20]{0:T(128)S(1)} %bitcast.20, ...), custom_call_target="tpu_custom_call" | custom-call | flops 17039360 | bytes 16777216 | tf_op jit(solution)/shard_map/pallas_call | solution.py:514
  10.1 0.0 collective-permute-done.halo_one
  10.1 0.0 collective-permute-done.2.halo_far
  10.2 0.0 collective-permute-done.1.halo_near
  10.2 0.0 copy-done.7
  10.2 7.5 %shard_map.88 = (s16[4,72,128]{2,1,0:T(8,128)(2,1)S(1)}, f32[600,128]{1,0:T(8,128)S(1)}) custom-call(s32[20]{0:T(128)S(1)} %bitcast.21, s32[20]{0:T(128)S(1)} %bitcast.23, s32[20]{0:T(128)S(1)} %bitcast.24, bf16[2,8,4096]{2,1,0:T(8,128)(2,1)S(1)} %collective-permute-done.halo_one, bf16[2,8,4096]{2,1,0:T(8,128)(2,1)S(1)} %collective-permute-done.1.halo_near, ...), custom_call_target="tpu_custom_call" | custom-call | tf_op jit(solution)/shard_map/pallas_call | solution.py:557
  17.7 0.1 collective-permute-start.3
  17.8 13.9 %all_to_all.5.received = s16[4,72,128]{2,1,0:T(8,128)(2,1)S(1)} all-to-all(s16[4,72,128]{2,1,0:T(8,128)(2,1)S(1)} %get-tuple-element.24), channel_id=1, replica_groups=mesh['section'=4,'frame'=2,'patch'=4] {'patch'}, dimensions={0} | all-to-all | bytes 147456 | tf_op jit(solution)/shard_map/all_to_all | solution.py:664
  31.7 0.0 collective-permute-done.3
  31.8 1.2 %shard_map.89 = (f32[20,25,1,50]{3,2,1,0:T(1,128)}, f32[25,20,50]{2,1,0:T(8,128)}) custom-call(s16[4,72,128]{2,1,0:T(8,128)(2,1)S(1)} %all_to_all.5.received, f32[600,128]{1,0:T(8,128)S(1)} %get-tuple-element.25.numer, f32[1,600,128]{2,1,0:T(8,128)S(1)} %bitcast.17), custom_call_target="tpu_custom_call" | custom-call | tf_op jit(solution)/shard_map/pallas_call | solution.py:594
  (5 shorter events, 0.0 us)
Async XLA Ops:
  0.6 1.2 %copy-start = (bf16[1,2,56,4096]{3,2,1,0:T(8,128)(2,1)S(1)}, bf16[1,2,56,4096]{3,2,1,0:T(8,128)(2,1)}, u32[]{:S(2)}) copy-start(bf16[1,2,56,4096]{3,2,1,0:T(8,128)(2,1)} %param.7) | copy-start | bytes 2752516
  1.8 4.6 %copy-start.1 = (bf16[1,2,56,4096]{3,2,1,0:T(8,128)(2,1)S(1)}, bf16[1,2,56,4096]{3,2,1,0:T(8,128)(2,1)}, u32[]{:S(2)}) copy-start(bf16[1,2,56,4096]{3,2,1,0:T(8,128)(2,1)} %param.7) | copy-start | bytes 2752516
  1.8 4.6 %copy-start.2 = (bf16[1,20,25,256]{3,1,2,0:T(8,128)(2,1)S(1)}, bf16[1,20,25,256]{3,1,2,0:T(8,128)(2,1)}, u32[]{:S(2)}) copy-start(bf16[1,20,25,256]{3,1,2,0:T(8,128)(2,1)} %param.9) | copy-start | bytes 768004
  1.8 4.6 %copy-start.3 = (bf16[1,20,50,64]{3,2,1,0:T(8,128)(2,1)S(1)}, bf16[1,20,50,64]{3,2,1,0:T(8,128)(2,1)}, u32[]{:S(2)}) copy-start(bf16[1,20,50,64]{3,2,1,0:T(8,128)(2,1)} %param.8) | copy-start | bytes 384004
  1.8 4.6 %copy-start.4 = (f32[1,20,25]{2,0,1:T(1,128)S(1)}, f32[1,20,25]{2,0,1:T(1,128)}, u32[]{:S(2)}) copy-start(f32[1,20,25]{2,0,1:T(1,128)} %param.13) | copy-start | bytes 6004
  1.8 4.6 %copy-start.5 = (s32[1,20]{1,0:T(1,128)S(1)}, s32[1,20]{1,0:T(1,128)}, u32[]{:S(2)}) copy-start(s32[1,20]{1,0:T(1,128)} %param.10) | copy-start | bytes 244
  1.8 4.6 %copy-start.6 = (s32[1,20]{1,0:T(1,128)S(1)}, s32[1,20]{1,0:T(1,128)}, u32[]{:S(2)}) copy-start(s32[1,20]{1,0:T(1,128)} %param.11) | copy-start | bytes 244
  1.8 8.3 %copy-start.7 = (s32[1,20]{1,0:T(1,128)S(1)}, s32[1,20]{1,0:T(1,128)}, u32[]{:S(2)}) copy-start(s32[1,20]{1,0:T(1,128)} %param.12) | copy-start | bytes 244
  1.9 8.2 %collective-permute-start = (bf16[2,8,4096]{2,1,0:T(8,128)(2,1)S(1)}, bf16[2,8,4096]{2,1,0:T(8,128)(2,1)S(1)}, u32[]{:S(2)}, u32[]{:S(2)}) collective-permute-start(bf16[2,8,4096]{2,1,0:T(8,128)(2,1)S(1)} %get-tuple-element.15), channel_id=1, source_target_pairs={{0,1},{2,3},{8,9},{10,11},{16,17},{18,19},{24,25},{26,27},{1,0},{3... | collective-permute-start | bytes 393224 | tf_op jit(solution)/shard_map/ppermute | solution.py:639
  5.0 5.1 %collective-permute-start.2 = (bf16[2,8,4096]{2,1,0:T(8,128)(2,1)S(1)}, bf16[2,8,4096]{2,1,0:T(8,128)(2,1)S(1)}, u32[]{:S(2)}, u32[]{:S(2)}) collective-permute-start(bf16[2,8,4096]{2,1,0:T(8,128)(2,1)S(1)} %get-tuple-element.16), channel_id=1, source_target_pairs={{3,8},{11,16},{19,24},{8,3},{16,11},{24,19},{7,12},{15,20},{23,28}... | collective-permute-start | bytes 393224 | tf_op jit(solution)/shard_map/ppermute | solution.py:639
  5.7 4.5 %collective-permute-start.1 = (bf16[2,8,4096]{2,1,0:T(8,128)(2,1)S(1)}, bf16[2,8,4096]{2,1,0:T(8,128)(2,1)S(1)}, u32[]{:S(2)}, u32[]{:S(2)}) collective-permute-start(bf16[2,8,4096]{2,1,0:T(8,128)(2,1)S(1)} %get-tuple-element.16), channel_id=1, source_target_pairs={{1,2},{9,10},{17,18},{25,26},{2,1},{10,9},{18,17},{26,25},{5,6},{1... | collective-permute-start | bytes 393224 | tf_op jit(solution)/shard_map/ppermute | solution.py:639
  17.7 14.0 %collective-permute-start.3 = (f32[600,128]{1,0:T(8,128)S(1)}, f32[600,128]{1,0:T(8,128)S(1)}, u32[]{:S(2)}, u32[]{:S(2)}) collective-permute-start(f32[600,128]{1,0:T(8,128)S(1)} %get-tuple-element.25.numer), channel_id=1, source_target_pairs={{0,4},{4,0},{1,5},{5,1},{2,6},{6,2},{3,7},{7,3},{8,12},{12,8},{9,1... | collective-permute-start | bytes 921608 | tf_op jit(solution)/shard_map/ppermute | solution.py:667

commit v4 on v3

--- a/solution.py
+++ b/solution.py
@@ -173,8 +173,8 @@
     col_off_in,
     dest_in,
     halo_one,
+    halo_far,
     halo_near,
-    halo_far,
     products,
     weights_w,
     upper_wx,
@@ -219,7 +219,7 @@
     rank = lax.axis_index("section") * lax.axis_size("patch") + lax.axis_index("patch")
     odd = lax.rem(rank, 2) == 1
 
-    for slot, sources in enumerate(((halo_one,), (halo_near, halo_far))):
+    for slot, sources in enumerate(((halo_one,), (halo_far, halo_near))):
         rows = slice(slot * HALO, (slot + 1) * HALO)
         values, inverse = (
             sum(source[channel].astype(F32) for source in sources) for channel in range(2)
@@ -641,7 +641,7 @@
     odd = range(1, count, 2)
     far = [i for i in odd if (i + 1) % group == 0]
     near = [i for i in odd if (i + 1) % group]
-    return [exchange(one, range(0, count, 2)), exchange(two, near), exchange(two, far)]
+    return [exchange(one, range(0, count, 2)), exchange(two, far), exchange(two, near)]
 
 
 def local(exposure, row_prof, col_prof, row_off, col_off, dest, fibre_weight):

time: 33.2 us -> 33.8 us (1.018)
  blocking collectives: 13.9 us -> 14.6 us
    all_to_all x1, blocking collectives: 13.9 us -> 14.6 us  [local(): lax.all_to_all(send, 'patch', split_axis=0, concat_axis=0, tiled=True)]
where the time goes in v4:
time: 33.8 us; the launch traced here: 33.6 us
  blocking collectives  14.6 us (43%)
  Pallas kernels  12.5 us (37%)
  starting transfers between devices  4.49 us (13%)
  local copies, waits for them, and re-layouts  1.2 us (4%)
  between operations  0.8 us (2%)
    all_to_all x1, blocking collectives, local(): lax.all_to_all(send, 'patch', split_axis=0, concat_axis=0, tiled=True)  14.6 us
    pallas_call x1, Pallas kernels, solve(): pl.pallas_call(functools.partial(solve_kernel, fibres, waves), out_shape=...  7.55 us
    ppermute x3, starting transfers between devices, exchange(): return lax.ppermute(value, axes, pairs + [(b, a) for a, b in pairs])  4.41 us
    pallas_call x1, Pallas kernels, prepare(): pl.pallas_call(prepare_kernel, out_shape=(made(rows, 2 * PC), made(PR, PC...  3.7 us
    unnamed x16, local copies, waits for them, and re-layouts  1.2 us
    pallas_call x1, Pallas kernels, finish(): pl.pallas_call(functools.partial(finish_kernel, capacity), out_shape=(jax...  1.19 us
  transfers between devices with their start and end apart: 4, of which 0 were waited for; matrix products, arithmetic and copies ran while one was open for 0% of the time, Pallas kernels for 11%

profile of v4, /device:TPU:0, one launch (start us, length us, event | category | flops | bytes accessed | tf_op | source)
XLA Modules:
  0.0 33.6 jit_solution(7720854710757245724)
XLA Ops:
  0.6 0.0 copy-start
  0.6 1.2 %copy-done = bf16[1,2,56,4096]{3,2,1,0:T(8,128)(2,1)S(1)} copy-done((bf16[1,2,56,4096]{3,2,1,0:T(8,128)(2,1)S(1)}, bf16[1,2,56,4096]{3,2,1,0:T(8,128)(2,1)}, u32[]{:S(2)}) %copy-start) | copy-done | bytes 917528
  1.8 0.0 copy-start.5
  1.8 0.0 copy-start.6
  1.8 0.0 copy-start.7
  1.9 0.1 shard_map.86
  1.9 3.1 %collective-permute-start = (bf16[2,8,4096]{2,1,0:T(8,128)(2,1)S(1)}, bf16[2,8,4096]{2,1,0:T(8,128)(2,1)S(1)}, u32[]{:S(2)}, u32[]{:S(2)}) collective-permute-start(bf16[2,8,4096]{2,1,0:T(8,128)(2,1)S(1)} %get-tuple-element.15), channel_id=1, source_target_pairs={{0,1},{2,3},{8,9},{10,11},{16,17},{18,19},{24,25},{26,27},{1,0},{3... | collective-permute-start | bytes 393224 | tf_op jit(solution)/shard_map/ppermute | solution.py:639
  5.0 0.7 %collective-permute-start.2 = (bf16[2,8,4096]{2,1,0:T(8,128)(2,1)S(1)}, bf16[2,8,4096]{2,1,0:T(8,128)(2,1)S(1)}, u32[]{:S(2)}, u32[]{:S(2)}) collective-permute-start(bf16[2,8,4096]{2,1,0:T(8,128)(2,1)S(1)} %get-tuple-element.16), channel_id=1, source_target_pairs={{1,2},{9,10},{17,18},{25,26},{2,1},{10,9},{18,17},{26,25},{5,6},{1... | collective-permute-start | bytes 393224 | tf_op jit(solution)/shard_map/ppermute | solution.py:639
  5.7 0.7 %collective-permute-start.1 = (bf16[2,8,4096]{2,1,0:T(8,128)(2,1)S(1)}, bf16[2,8,4096]{2,1,0:T(8,128)(2,1)S(1)}, u32[]{:S(2)}, u32[]{:S(2)}) collective-permute-start(bf16[2,8,4096]{2,1,0:T(8,128)(2,1)S(1)} %get-tuple-element.16), channel_id=1, source_target_pairs={{3,8},{11,16},{19,24},{8,3},{16,11},{24,19},{7,12},{15,20},{23,28}... | collective-permute-start | bytes 393224 | tf_op jit(solution)/shard_map/ppermute | solution.py:639
  6.4 0.0 copy-done.1
  6.4 0.0 copy-done.2
  6.4 0.0 copy-done.3
  6.4 0.0 copy-done.4
  6.4 0.0 copy-done.5
  6.4 3.7 %shard_map.87 = (bf16[20,416,512]{2,1,0:T(8,128)(2,1)S(1)}, bf16[20,64,256]{2,1,0:T(8,128)(2,1)S(1)}, bf16[20,64,256]{2,1,0:T(8,128)(2,1)S(1)}, bf16[20,64,256]{...) custom-call(s32[20]{0:T(128)S(1)} %bitcast.20, ...), custom_call_target="tpu_custom_call" | custom-call | flops 17039360 | bytes 16777216 | tf_op jit(solution)/shard_map/pallas_call | solution.py:514
  10.1 0.0 collective-permute-done.halo_one
  10.1 0.0 collective-permute-done.2.halo_near
  10.2 0.0 collective-permute-done.1.halo_far
  10.2 0.0 copy-done.7
  10.2 7.5 %shard_map.88 = (s16[4,72,128]{2,1,0:T(8,128)(2,1)S(1)}, f32[600,128]{1,0:T(8,128)S(1)}) custom-call(s32[20]{0:T(128)S(1)} %bitcast.21, s32[20]{0:T(128)S(1)} %bitcast.23, s32[20]{0:T(128)S(1)} %bitcast.24, bf16[2,8,4096]{2,1,0:T(8,128)(2,1)S(1)} %collective-permute-done.halo_one, bf16[2,8,4096]{2,1,0:T(8,128)(2,1)S(1)} %collective-permute-done.1.halo_far, ...), custom_call_target="tpu_custom_call" | custom-call | tf_op jit(solution)/shard_map/pallas_call | solution.py:557
  17.7 0.1 collective-permute-start.3
  17.8 14.6 %all_to_all.5.received = s16[4,72,128]{2,1,0:T(8,128)(2,1)S(1)} all-to-all(s16[4,72,128]{2,1,0:T(8,128)(2,1)S(1)} %get-tuple-element.24), channel_id=1, replica_groups=mesh['section'=4,'frame'=2,'patch'=4] {'patch'}, dimensions={0} | all-to-all | bytes 147456 | tf_op jit(solution)/shard_map/all_to_all | solution.py:664
  32.4 0.0 collective-permute-done.3
  32.4 1.2 %shard_map.89 = (f32[20,25,1,50]{3,2,1,0:T(1,128)}, f32[25,20,50]{2,1,0:T(8,128)}) custom-call(s16[4,72,128]{2,1,0:T(8,128)(2,1)S(1)} %all_to_all.5.received, f32[600,128]{1,0:T(8,128)S(1)} %get-tuple-element.25.numer, f32[1,600,128]{2,1,0:T(8,128)S(1)} %bitcast.17), custom_call_target="tpu_custom_call" | custom-call | tf_op jit(solution)/shard_map/pallas_call | solution.py:594
  (5 shorter events, 0.0 us)
Async XLA Ops:
  0.6 1.2 %copy-start = (bf16[1,2,56,4096]{3,2,1,0:T(8,128)(2,1)S(1)}, bf16[1,2,56,4096]{3,2,1,0:T(8,128)(2,1)}, u32[]{:S(2)}) copy-start(bf16[1,2,56,4096]{3,2,1,0:T(8,128)(2,1)} %param.7) | copy-start | bytes 2752516
  1.8 4.6 %copy-start.1 = (bf16[1,2,56,4096]{3,2,1,0:T(8,128)(2,1)S(1)}, bf16[1,2,56,4096]{3,2,1,0:T(8,128)(2,1)}, u32[]{:S(2)}) copy-start(bf16[1,2,56,4096]{3,2,1,0:T(8,128)(2,1)} %param.7) | copy-start | bytes 2752516
  1.8 4.6 %copy-start.2 = (bf16[1,20,25,256]{3,1,2,0:T(8,128)(2,1)S(1)}, bf16[1,20,25,256]{3,1,2,0:T(8,128)(2,1)}, u32[]{:S(2)}) copy-start(bf16[1,20,25,256]{3,1,2,0:T(8,128)(2,1)} %param.9) | copy-start | bytes 768004
  1.8 4.6 %copy-start.3 = (bf16[1,20,50,64]{3,2,1,0:T(8,128)(2,1)S(1)}, bf16[1,20,50,64]{3,2,1,0:T(8,128)(2,1)}, u32[]{:S(2)}) copy-start(bf16[1,20,50,64]{3,2,1,0:T(8,128)(2,1)} %param.8) | copy-start | bytes 384004
  1.8 4.6 %copy-start.4 = (f32[1,20,25]{2,0,1:T(1,128)S(1)}, f32[1,20,25]{2,0,1:T(1,128)}, u32[]{:S(2)}) copy-start(f32[1,20,25]{2,0,1:T(1,128)} %param.13) | copy-start | bytes 6004
  1.8 4.6 %copy-start.5 = (s32[1,20]{1,0:T(1,128)S(1)}, s32[1,20]{1,0:T(1,128)}, u32[]{:S(2)}) copy-start(s32[1,20]{1,0:T(1,128)} %param.10) | copy-start | bytes 244
  1.8 4.6 %copy-start.6 = (s32[1,20]{1,0:T(1,128)S(1)}, s32[1,20]{1,0:T(1,128)}, u32[]{:S(2)}) copy-start(s32[1,20]{1,0:T(1,128)} %param.11) | copy-start | bytes 244
  1.8 8.3 %copy-start.7 = (s32[1,20]{1,0:T(1,128)S(1)}, s32[1,20]{1,0:T(1,128)}, u32[]{:S(2)}) copy-start(s32[1,20]{1,0:T(1,128)} %param.12) | copy-start | bytes 244
  1.9 8.2 %collective-permute-start = (bf16[2,8,4096]{2,1,0:T(8,128)(2,1)S(1)}, bf16[2,8,4096]{2,1,0:T(8,128)(2,1)S(1)}, u32[]{:S(2)}, u32[]{:S(2)}) collective-permute-start(bf16[2,8,4096]{2,1,0:T(8,128)(2,1)S(1)} %get-tuple-element.15), channel_id=1, source_target_pairs={{0,1},{2,3},{8,9},{10,11},{16,17},{18,19},{24,25},{26,27},{1,0},{3... | collective-permute-start | bytes 393224 | tf_op jit(solution)/shard_map/ppermute | solution.py:639
  5.0 5.1 %collective-permute-start.2 = (bf16[2,8,4096]{2,1,0:T(8,128)(2,1)S(1)}, bf16[2,8,4096]{2,1,0:T(8,128)(2,1)S(1)}, u32[]{:S(2)}, u32[]{:S(2)}) collective-permute-start(bf16[2,8,4096]{2,1,0:T(8,128)(2,1)S(1)} %get-tuple-element.16), channel_id=1, source_target_pairs={{1,2},{9,10},{17,18},{25,26},{2,1},{10,9},{18,17},{26,25},{5,6},{1... | collective-permute-start | bytes 393224 | tf_op jit(solution)/shard_map/ppermute | solution.py:639
  5.7 4.5 %collective-permute-start.1 = (bf16[2,8,4096]{2,1,0:T(8,128)(2,1)S(1)}, bf16[2,8,4096]{2,1,0:T(8,128)(2,1)S(1)}, u32[]{:S(2)}, u32[]{:S(2)}) collective-permute-start(bf16[2,8,4096]{2,1,0:T(8,128)(2,1)S(1)} %get-tuple-element.16), channel_id=1, source_target_pairs={{3,8},{11,16},{19,24},{8,3},{16,11},{24,19},{7,12},{15,20},{23,28}... | collective-permute-start | bytes 393224 | tf_op jit(solution)/shard_map/ppermute | solution.py:639
  17.7 14.7 %collective-permute-start.3 = (f32[600,128]{1,0:T(8,128)S(1)}, f32[600,128]{1,0:T(8,128)S(1)}, u32[]{:S(2)}, u32[]{:S(2)}) collective-permute-start(f32[600,128]{1,0:T(8,128)S(1)} %get-tuple-element.25.numer), channel_id=1, source_target_pairs={{0,4},{4,0},{1,5},{5,1},{2,6},{6,2},{3,7},{7,3},{8,12},{12,8},{9,1... | collective-permute-start | bytes 921608 | tf_op jit(solution)/shard_map/ppermute | solution.py:667

commit v5 on v3

--- a/solution.py
+++ b/solution.py
@@ -231,8 +231,10 @@
     partial[...] = jnp.zeros_like(partial)
     halo_row = lax.broadcasted_iota(jnp.int32, (HALO, LANES), 0)
     empty = jnp.zeros((PR, PC), BF16)
-    copies[0].wait()
-    copies[1].wait()
+    packed[...] = jnp.zeros_like(packed)
+    numer[...] = jnp.zeros_like(numer)
+    for copy in copies:
+        copy.wait()
 
     def beside_own(edge, own):
         return jnp.concatenate([edge, own.astype(F32)[HALO:]], axis=0).astype(BF16)
@@ -399,16 +401,15 @@
             direction[pair] = residual[pair] + ratio[row : row + 1] * direction[pair]
         norm[half] = norm_next
 
-    copies[2].wait()
-    for index in range(send.shape[0]):
-        counts[index] = 0
-    for patch in range(patches):
-        target = dest[patch]
-        slot = counts[target]
-        counts[target] = slot + 1
-        slots[patch] = slot
-    packed[...] = jnp.zeros_like(packed)
-    numer[...] = jnp.zeros_like(numer)
+    def number_slots():
+        for index in range(send.shape[0]):
+            counts[index] = 0
+        for patch in range(patches):
+            target = dest[patch]
+            slot = counts[target]
+            counts[target] = slot + 1
+            slots[patch] = slot
+
     upper_rows = (fibres + 1) // 2
     lane_f = lax.broadcasted_iota(jnp.int32, (padded_f, LANES), 1)
     at_wave = lax.rem(lane_f, HALF) == waves
@@ -453,6 +454,7 @@
         move(1)
         image(1)
         move(0)
+    number_slots()
     image(0, folded=False)
     move(1)
     advance(0)

time: 33.2 us -> 33.1 us (level)
  no operation moved by 1% of the time
where the time goes in v5:
time: 33.1 us; the launch traced here: 32.9 us
  blocking collectives  13.9 us (42%)
  Pallas kernels  12.4 us (37%)
  starting transfers between devices  4.49 us (14%)
  local copies, waits for them, and re-layouts  1.2 us (4%)
  between operations  0.8 us (2%)
    all_to_all x1, blocking collectives, local(): lax.all_to_all(send, 'patch', split_axis=0, concat_axis=0, tiled=True)  13.9 us
    pallas_call x1, Pallas kernels, solve(): pl.pallas_call(functools.partial(solve_kernel, fibres, waves), out_shape=...  7.47 us
    ppermute x3, starting transfers between devices, exchange(): return lax.ppermute(value, axes, pairs + [(b, a) for a, b in pairs])  4.41 us
    pallas_call x1, Pallas kernels, prepare(): pl.pallas_call(prepare_kernel, out_shape=(made(rows, 2 * PC), made(PR, PC...  3.7 us
    unnamed x16, local copies, waits for them, and re-layouts  1.2 us
    pallas_call x1, Pallas kernels, finish(): pl.pallas_call(functools.partial(finish_kernel, capacity), out_shape=(jax...  1.19 us
  transfers between devices with their start and end apart: 4, of which 0 were waited for; matrix products, arithmetic and copies ran while one was open for 0% of the time, Pallas kernels for 11%

profile of v5, /device:TPU:0, one launch (start us, length us, event | category | flops | bytes accessed | tf_op | source)
XLA Modules:
  0.0 32.9 jit_solution(7722705999282932157)
XLA Ops:
  0.6 0.0 copy-start
  0.6 1.2 %copy-done = bf16[1,2,56,4096]{3,2,1,0:T(8,128)(2,1)S(1)} copy-done((bf16[1,2,56,4096]{3,2,1,0:T(8,128)(2,1)S(1)}, bf16[1,2,56,4096]{3,2,1,0:T(8,128)(2,1)}, u32[]{:S(2)}) %copy-start) | copy-done | bytes 917528
  1.8 0.0 copy-start.5
  1.8 0.0 copy-start.6
  1.8 0.0 copy-start.7
  1.9 0.1 shard_map.86
  1.9 3.1 %collective-permute-start = (bf16[2,8,4096]{2,1,0:T(8,128)(2,1)S(1)}, bf16[2,8,4096]{2,1,0:T(8,128)(2,1)S(1)}, u32[]{:S(2)}, u32[]{:S(2)}) collective-permute-start(bf16[2,8,4096]{2,1,0:T(8,128)(2,1)S(1)} %get-tuple-element.15), channel_id=1, source_target_pairs={{0,1},{2,3},{8,9},{10,11},{16,17},{18,19},{24,25},{26,27},{1,0},{3... | collective-permute-start | bytes 393224 | tf_op jit(solution)/shard_map/ppermute | solution.py:641
  5.0 0.7 %collective-permute-start.2 = (bf16[2,8,4096]{2,1,0:T(8,128)(2,1)S(1)}, bf16[2,8,4096]{2,1,0:T(8,128)(2,1)S(1)}, u32[]{:S(2)}, u32[]{:S(2)}) collective-permute-start(bf16[2,8,4096]{2,1,0:T(8,128)(2,1)S(1)} %get-tuple-element.16), channel_id=1, source_target_pairs={{3,8},{11,16},{19,24},{8,3},{16,11},{24,19},{7,12},{15,20},{23,28}... | collective-permute-start | bytes 393224 | tf_op jit(solution)/shard_map/ppermute | solution.py:641
  5.7 0.7 %collective-permute-start.1 = (bf16[2,8,4096]{2,1,0:T(8,128)(2,1)S(1)}, bf16[2,8,4096]{2,1,0:T(8,128)(2,1)S(1)}, u32[]{:S(2)}, u32[]{:S(2)}) collective-permute-start(bf16[2,8,4096]{2,1,0:T(8,128)(2,1)S(1)} %get-tuple-element.16), channel_id=1, source_target_pairs={{1,2},{9,10},{17,18},{25,26},{2,1},{10,9},{18,17},{26,25},{5,6},{1... | collective-permute-start | bytes 393224 | tf_op jit(solution)/shard_map/ppermute | solution.py:641
  6.4 0.0 copy-done.1
  6.4 0.0 copy-done.2
  6.4 0.0 copy-done.3
  6.4 0.0 copy-done.4
  6.4 0.0 copy-done.5
  6.4 0.0 copy-done.6
  6.4 3.7 %shard_map.87 = (bf16[20,416,512]{2,1,0:T(8,128)(2,1)S(1)}, bf16[20,64,256]{2,1,0:T(8,128)(2,1)S(1)}, bf16[20,64,256]{2,1,0:T(8,128)(2,1)S(1)}, bf16[20,64,256]{...) custom-call(s32[20]{0:T(128)S(1)} %bitcast.20, ...), custom_call_target="tpu_custom_call" | custom-call | flops 17039360 | bytes 16777216 | tf_op jit(solution)/shard_map/pallas_call | solution.py:516
  10.1 0.0 collective-permute-done.halo_one
  10.1 0.0 collective-permute-done.2.halo_far
  10.2 0.0 collective-permute-done.1.halo_near
  10.2 7.5 %shard_map.88 = (s16[4,72,128]{2,1,0:T(8,128)(2,1)S(1)}, f32[600,128]{1,0:T(8,128)S(1)}) custom-call(s32[20]{0:T(128)S(1)} %bitcast.21, s32[20]{0:T(128)S(1)} %bitcast.23, s32[20]{0:T(128)S(1)} %bitcast.24, bf16[2,8,4096]{2,1,0:T(8,128)(2,1)S(1)} %collective-permute-done.halo_one, bf16[2,8,4096]{2,1,0:T(8,128)(2,1)S(1)} %collective-permute-done.1.halo_near, ...), custom_call_target="tpu_custom_call" | custom-call | tf_op jit(solution)/shard_map/pallas_call | solution.py:559
  17.7 0.1 collective-permute-start.3
  17.7 13.9 %all_to_all.5.received = s16[4,72,128]{2,1,0:T(8,128)(2,1)S(1)} all-to-all(s16[4,72,128]{2,1,0:T(8,128)(2,1)S(1)} %get-tuple-element.24), channel_id=1, replica_groups=mesh['section'=4,'frame'=2,'patch'=4] {'patch'}, dimensions={0} | all-to-all | bytes 147456 | tf_op jit(solution)/shard_map/all_to_all | solution.py:666
  31.7 0.0 collective-permute-done.3
  31.7 1.2 %shard_map.89 = (f32[20,25,1,50]{3,2,1,0:T(1,128)}, f32[25,20,50]{2,1,0:T(8,128)}) custom-call(s16[4,72,128]{2,1,0:T(8,128)(2,1)S(1)} %all_to_all.5.received, f32[600,128]{1,0:T(8,128)S(1)} %get-tuple-element.25.numer, f32[1,600,128]{2,1,0:T(8,128)S(1)} %bitcast.17), custom_call_target="tpu_custom_call" | custom-call | tf_op jit(solution)/shard_map/pallas_call | solution.py:596
  (5 shorter events, 0.0 us)
Async XLA Ops:
  0.6 1.2 %copy-start = (bf16[1,2,56,4096]{3,2,1,0:T(8,128)(2,1)S(1)}, bf16[1,2,56,4096]{3,2,1,0:T(8,128)(2,1)}, u32[]{:S(2)}) copy-start(bf16[1,2,56,4096]{3,2,1,0:T(8,128)(2,1)} %param.7) | copy-start | bytes 2752516
  1.8 4.6 %copy-start.1 = (bf16[1,2,56,4096]{3,2,1,0:T(8,128)(2,1)S(1)}, bf16[1,2,56,4096]{3,2,1,0:T(8,128)(2,1)}, u32[]{:S(2)}) copy-start(bf16[1,2,56,4096]{3,2,1,0:T(8,128)(2,1)} %param.7) | copy-start | bytes 2752516
  1.8 4.6 %copy-start.2 = (bf16[1,20,25,256]{3,1,2,0:T(8,128)(2,1)S(1)}, bf16[1,20,25,256]{3,1,2,0:T(8,128)(2,1)}, u32[]{:S(2)}) copy-start(bf16[1,20,25,256]{3,1,2,0:T(8,128)(2,1)} %param.9) | copy-start | bytes 768004
  1.8 4.6 %copy-start.3 = (bf16[1,20,50,64]{3,2,1,0:T(8,128)(2,1)S(1)}, bf16[1,20,50,64]{3,2,1,0:T(8,128)(2,1)}, u32[]{:S(2)}) copy-start(bf16[1,20,50,64]{3,2,1,0:T(8,128)(2,1)} %param.8) | copy-start | bytes 384004
  1.8 4.6 %copy-start.4 = (f32[1,20,25]{2,0,1:T(1,128)S(1)}, f32[1,20,25]{2,0,1:T(1,128)}, u32[]{:S(2)}) copy-start(f32[1,20,25]{2,0,1:T(1,128)} %param.13) | copy-start | bytes 6004
  1.8 4.6 %copy-start.5 = (s32[1,20]{1,0:T(1,128)S(1)}, s32[1,20]{1,0:T(1,128)}, u32[]{:S(2)}) copy-start(s32[1,20]{1,0:T(1,128)} %param.10) | copy-start | bytes 244
  1.8 4.6 %copy-start.6 = (s32[1,20]{1,0:T(1,128)S(1)}, s32[1,20]{1,0:T(1,128)}, u32[]{:S(2)}) copy-start(s32[1,20]{1,0:T(1,128)} %param.11) | copy-start | bytes 244
  1.8 8.3 %copy-start.7 = (s32[1,20]{1,0:T(1,128)S(1)}, s32[1,20]{1,0:T(1,128)}, u32[]{:S(2)}) copy-start(s32[1,20]{1,0:T(1,128)} %param.12) | copy-start | bytes 244
  1.9 8.2 %collective-permute-start = (bf16[2,8,4096]{2,1,0:T(8,128)(2,1)S(1)}, bf16[2,8,4096]{2,1,0:T(8,128)(2,1)S(1)}, u32[]{:S(2)}, u32[]{:S(2)}) collective-permute-start(bf16[2,8,4096]{2,1,0:T(8,128)(2,1)S(1)} %get-tuple-element.15), channel_id=1, source_target_pairs={{0,1},{2,3},{8,9},{10,11},{16,17},{18,19},{24,25},{26,27},{1,0},{3... | collective-permute-start | bytes 393224 | tf_op jit(solution)/shard_map/ppermute | solution.py:641
  5.0 5.1 %collective-permute-start.2 = (bf16[2,8,4096]{2,1,0:T(8,128)(2,1)S(1)}, bf16[2,8,4096]{2,1,0:T(8,128)(2,1)S(1)}, u32[]{:S(2)}, u32[]{:S(2)}) collective-permute-start(bf16[2,8,4096]{2,1,0:T(8,128)(2,1)S(1)} %get-tuple-element.16), channel_id=1, source_target_pairs={{3,8},{11,16},{19,24},{8,3},{16,11},{24,19},{7,12},{15,20},{23,28}... | collective-permute-start | bytes 393224 | tf_op jit(solution)/shard_map/ppermute | solution.py:641
  5.7 4.5 %collective-permute-start.1 = (bf16[2,8,4096]{2,1,0:T(8,128)(2,1)S(1)}, bf16[2,8,4096]{2,1,0:T(8,128)(2,1)S(1)}, u32[]{:S(2)}, u32[]{:S(2)}) collective-permute-start(bf16[2,8,4096]{2,1,0:T(8,128)(2,1)S(1)} %get-tuple-element.16), channel_id=1, source_target_pairs={{1,2},{9,10},{17,18},{25,26},{2,1},{10,9},{18,17},{26,25},{5,6},{1... | collective-permute-start | bytes 393224 | tf_op jit(solution)/shard_map/ppermute | solution.py:641
  17.7 14.0 %collective-permute-start.3 = (f32[600,128]{1,0:T(8,128)S(1)}, f32[600,128]{1,0:T(8,128)S(1)}, u32[]{:S(2)}, u32[]{:S(2)}) collective-permute-start(f32[600,128]{1,0:T(8,128)S(1)} %get-tuple-element.25.numer), channel_id=1, source_target_pairs={{0,4},{4,0},{1,5},{5,1},{2,6},{6,2},{3,7},{7,3},{8,12},{12,8},{9,1... | collective-permute-start | bytes 921608 | tf_op jit(solution)/shard_map/ppermute | solution.py:669
